TPU v7x, 128 devices: a whole 4x4x4 slice. The times are simulated.
128 devices in a mesh: dp: 16 (over x, y), mp: 8 (over z, core).
Axes of the slice: x: 4, y: 4, z: 4, core: 2. Of those that a mesh axis runs over, the one named last changes fastest.
Arguments:
- tokens: bfloat16 [6144, 8192], P('dp', 'mp'), may hold values from -6 to 6
- cotangent: bfloat16 [6144, 8192], P('dp', 'mp'), may hold values from -1.5 to 1.5
- token_adapter_index: int32 [6144, 1], P('dp'), may hold values from 0 to 127; in each aligned block of 384 rows (0 to 383, 384 to 767, ...) at most 6 rows name the same one
- adapter_storage_row: int32 [128], replicated, may hold values from 0 to 127, each once
- frozen_weight_matrix: bfloat16 [8192, 8192], P(None, 'mp'), may hold values from -0.0625 to 0.0625
- first_adapter_factors: bfloat16 [128, 64, 8192], P('dp', None, 'mp'), may hold values from -0.0625 to 0.0625
- second_adapter_factors: bfloat16 [128, 64, 8192], P('dp', None, 'mp'), may hold values from -0.0625 to 0.0625
Outputs:
- output: bfloat16 [6144, 8192], P('dp', 'mp')
- input_gradient: bfloat16 [6144, 8192], P(('dp', 'mp'))
- first_factor_gradient: float32 [128, 64, 8192], P('dp', None, 'mp')
- second_factor_gradient: float32 [128, 64, 8192], P('dp', None, 'mp')
Inputs may be any that keep to these rules, and one draw needn't show every extreme that they name: `token_adapter_index`: in the rows of one device no adapter is named by more than 6 rows, a bound that some block reaches. `adapter_storage_row`: each adapter has its own storage row.
All inputs are finite; a program needn't handle non-finite values.
Results may differ from a plain program's by a relative error of at most 0.019.
Values may be sent and summed in bfloat16 or wider, within the bound.
A program may use at most 128 MiB of HBM per device.

v0:
```python
import jax
import jax.numpy as jnp
from jax import lax
from jax.sharding import PartitionSpec as P

adapter_scale = 2.0


def local(
    tokens,
    cotangent,
    token_adapter_index,
    adapter_storage_row,
    frozen_weight_matrix,
    first_adapter_factors,
    second_adapter_factors,
):
    tok_rows = tokens.shape[0]
    column_values = tokens.shape[1]
    rank_dimension = first_adapter_factors.shape[1]
    dp_count = lax.axis_size("dp")
    resident_adapters = first_adapter_factors.shape[0]
    adapters = resident_adapters * dp_count
    capacity = max(2, 2 * tok_rows // adapters)
    catalog = jnp.arange(adapters, dtype=jnp.int32)
    id_match = (token_adapter_index[:, 0][:, None] == catalog[None, :]).astype(jnp.int32)
    storage = jnp.sum(id_match * adapter_storage_row[None, :], axis=1)
    onehot = (storage[:, None] == catalog[None, :]).astype(jnp.int32)
    position = jnp.sum((jnp.cumsum(onehot, axis=0) - onehot) * onehot, axis=1)
    destination = storage * capacity + position
    frozen_out = jnp.dot(
        lax.all_gather(tokens, "mp", axis=1, tiled=True),
        frozen_weight_matrix,
        preferred_element_type=jnp.float32,
    )
    blank = jnp.zeros((adapters * capacity, column_values), jnp.bfloat16)
    send_x = blank.at[destination].set(tokens)
    send_g = blank.at[destination].set(cotangent)
    received_input = lax.all_to_all(send_x, "dp", split_axis=0, concat_axis=0, tiled=True)
    received_gradient = lax.all_to_all(send_g, "dp", split_axis=0, concat_axis=0, tiled=True)
    shape_four = (dp_count, resident_adapters, capacity, column_values)
    received_input = received_input.reshape(shape_four)
    received_gradient = received_gradient.reshape(shape_four)
    down_projection_piece = jnp.einsum(
        "fepn,ehn->feph", received_input, first_adapter_factors, preferred_element_type=jnp.float32
    )
    gradient_piece = jnp.einsum(
        "fepn,ehn->feph",
        received_gradient,
        second_adapter_factors,
        preferred_element_type=jnp.float32,
    )
    flat_shape = (dp_count * resident_adapters, capacity * rank_dimension)
    down_sum, grad_sum = (
        lax.psum(down_projection_piece.reshape(flat_shape).astype(jnp.bfloat16), "mp").astype(
            jnp.float32
        ),
        lax.psum(gradient_piece.reshape(flat_shape).astype(jnp.bfloat16), "mp").astype(jnp.float32),
    )
    rank_shape = (dp_count, resident_adapters, capacity, rank_dimension)
    down_rank_values = down_sum.reshape(rank_shape).astype(jnp.bfloat16)
    gradient_rank_values = grad_sum.reshape(rank_shape).astype(jnp.bfloat16)
    adapter_output = adapter_scale * jnp.einsum(
        "imtj,mjq->imtq",
        down_rank_values,
        second_adapter_factors,
        preferred_element_type=jnp.float32,
    )
    back_out = lax.all_to_all(
        adapter_output.astype(jnp.bfloat16).reshape(-1, column_values),
        "dp",
        split_axis=0,
        concat_axis=0,
        tiled=True,
    )
    adapter_backward = adapter_scale * jnp.einsum(
        "imtj,mjq->imtq",
        gradient_rank_values,
        first_adapter_factors,
        preferred_element_type=jnp.float32,
    )
    backward_returned = lax.all_to_all(
        adapter_backward.astype(jnp.bfloat16).reshape(-1, column_values),
        "dp",
        split_axis=0,
        concat_axis=0,
        tiled=True,
    )
    output = (frozen_out + back_out[destination].astype(jnp.float32)).astype(jnp.bfloat16)
    second_factor_gradient = adapter_scale * jnp.einsum(
        "sacr,sacd->ard", down_rank_values, received_gradient, preferred_element_type=jnp.float32
    )
    first_factor_gradient = adapter_scale * jnp.einsum(
        "sacr,sacd->ard", gradient_rank_values, received_input, preferred_element_type=jnp.float32
    )
    adapter_row_values = backward_returned[destination]
    adapter_piece = lax.all_to_all(
        adapter_row_values, "mp", split_axis=0, concat_axis=1, tiled=True
    )
    frozen_backward = lax.psum_scatter(
        lax.dot_general(
            cotangent,
            frozen_weight_matrix,
            (((1,), (1,)), ((), ())),
            preferred_element_type=jnp.float32,
        ).astype(jnp.bfloat16),
        "mp",
        scatter_dimension=0,
        tiled=True,
    ).astype(jnp.float32)
    input_gradient = (frozen_backward + adapter_piece.astype(jnp.float32)).astype(jnp.bfloat16)
    return (output, input_gradient, first_factor_gradient, second_factor_gradient)


def solution(mesh):
    in_specs = (
        P("dp", "mp"),
        P("dp", "mp"),
        P("dp", None),
        P(),
        P(None, "mp"),
        P("dp", None, "mp"),
        P("dp", None, "mp"),
    )
    out_specs = (P("dp", "mp"), P(("dp", "mp"), None), P("dp", None, "mp"), P("dp", None, "mp"))
    return jax.shard_map(local, mesh=mesh, in_specs=in_specs, out_specs=out_specs, check_vma=False)
```

profile of v0, /device:TPU:1, one launch (start us, length us, event | category | flops | bytes accessed | tf_op | source)
XLA Modules:
  0.0 242.8 jit_solution(11442503003085243441)
XLA Ops:
  7.2 0.0 copy-start
  7.2 0.8 reduce
  8.0 0.9 select_reduce_fusion
  8.8 0.1 copy.21
  9.0 0.2 fusion.10
  9.2 0.1 broadcast_add_fusion
  9.3 0.2 fusion.13
  9.6 4.0 %scatter_custom_fusion = bf16[768,1024]{1,0:T(8,128)(2,1)} fusion(s32[384]{0:T(512)S(1)} %fusion.15, bf16[384,1024]{1,0:T(8,128)(2,1)} %param.7, bf16[]{:T(256)} %constant.5.clone.1), kind=kCustom, calls=%fused_computation.22 | custom fusion | bytes 1573376 | tf_op jit(solution)/shard_map/scatter | solution.py:37
  13.5 7.6 %all-to-all-start = ((bf16[16,48,1024]{2,1,0:T(8,128)(2,1)}), bf16[16,48,1024]{2,1,0:T(8,128)(2,1)S(1)}, u32[]{:S(2)}, u32[]{:S(2)}) async-start(bf16[16,48,1024]{2,1,0:T(8,128)(2,1)} %bitcast.69), calls=%async_computation | async-start | bytes 3145728 | tf_op jit(solution)/shard_map/all_to_all | solution.py:39
  21.1 4.0 %scatter_custom_fusion.1 = bf16[768,1024]{1,0:T(8,128)(2,1)} fusion(s32[384]{0:T(512)S(1)} %fusion.15, bf16[384,1024]{1,0:T(8,128)(2,1)} %param.8, bf16[]{:T(256)} %constant.5.clone.1), kind=kCustom, calls=%fused_computation.20 | custom fusion | bytes 1573376 | tf_op jit(solution)/shard_map/scatter | solution.py:38
  25.1 16.7 %all-to-all-done = bf16[16,48,1024]{2,1,0:T(8,128)(2,1)S(1)} async-done(((bf16[16,48,1024]{2,1,0:T(8,128)(2,1)}), bf16[16,48,1024]{2,1,0:T(8,128)(2,1)S(1)}, u32[]{:S(2)}, u32[]{:S(2)}) %all-to-all-start) | async-done | bytes 1572896 | tf_op jit(solution)/shard_map/all_to_all | solution.py:39
  41.8 5.4 %all-to-all-start.2 = ((bf16[16,48,1024]{2,1,0:T(8,128)(2,1)}), bf16[16,48,1024]{2,1,0:T(8,128)(2,1)}, u32[]{:S(2)}, u32[]{:S(2)}) async-start(bf16[16,48,1024]{2,1,0:T(8,128)(2,1)} %bitcast.67), calls=%async_computation.3 | async-start | bytes 3145728 | tf_op jit(solution)/shard_map/all_to_all | solution.py:40
  47.1 0.0 all-reduce.3.cloned.1.call-start
  47.2 0.9 copy.23
  48.1 1.2 copy-done.2
  49.3 1.2 fusion
  50.5 16.5 %all-to-all-done.2 = bf16[16,48,1024]{2,1,0:T(8,128)(2,1)} async-done(((bf16[16,48,1024]{2,1,0:T(8,128)(2,1)}), bf16[16,48,1024]{2,1,0:T(8,128)(2,1)}, u32[]{:S(2)}, u32[]{:S(2)}) %all-to-all-start.2) | async-done | bytes 1572896 | tf_op jit(solution)/shard_map/all_to_all | solution.py:40
  67.0 2.3 copy.25
  69.3 1.1 copy-done.4
  70.4 1.2 fusion.1
  71.7 0.0 all-reduce.3.cloned.1.call-update
  71.7 0.0 all-gather.2.cloned.1.call-start
  71.8 0.7 all-gather.2.cloned.1.call-update
  72.5 0.2 reduce-scatter.2.cloned.1.call-start
  72.7 12.2 %convolution_convert_fusion = bf16[384,8192]{1,0:T(8,128)(2,1)} fusion(bf16[384,1024]{1,0:T(8,128)(2,1)} %param.8, bf16[8192,1024]{1,0:T(8,128)(2,1)} %param.11), kind=kOutput, calls=%fused_computation.4 | convolution fusion | flops 6445596672 | bytes 23855104 | tf_op jit(solution)/shard_map/dot_general | solution.py:101
  84.9 0.0 reduce-scatter.2.cloned.1.call-update
  84.9 48.5 %all-reduce.3.cloned.1.call-done = (bf16[16,8,6,64]{3,0,2,1:T(8,128)(2,1)}, bf16[16,8,6,64]{3,0,2,1:T(8,128)(2,1)}) async-done(((bf16[16,8,6,64]{3,0,2,1:T(8,128)(2,1)}, bf16[16,8,6,64]{3,0,2,1:T(8,128)(2,1)}), (bf16[16,8,6,64]{3,0,2,1:T(8,128)(2,1)}, bf16[16,8,6,64]{3,0,2,1:T(8,128)(2,1)})) %all-reduce.3.cloned.1.call-update) | async-done | bytes 196624 | tf_op jit(solution)/shard_map/psum | solution.py:55
  133.4 1.5 multiply_convert_fusion
  134.9 2.0 copy.26
  136.9 6.7 %all-to-all-start.3 = ((bf16[16,48,1024]{2,1,0:T(8,128)(2,1)}), bf16[16,48,1024]{2,1,0:T(8,128)(2,1)S(1)}, u32[]{:S(2)}, u32[]{:S(2)}) async-start(bf16[16,48,1024]{2,1,0:T(8,128)(2,1)} %copy.26), calls=%async_computation.4 | async-start | bytes 3145728 | tf_op jit(solution)/shard_map/all_to_all | solution.py:82
  143.6 1.8 multiply_convert_fusion.1
  145.4 2.0 copy.24
  147.4 16.1 %all-to-all-done.3 = bf16[16,48,1024]{2,1,0:T(8,128)(2,1)S(1)} async-done(((bf16[16,48,1024]{2,1,0:T(8,128)(2,1)}), bf16[16,48,1024]{2,1,0:T(8,128)(2,1)S(1)}, u32[]{:S(2)}, u32[]{:S(2)}) %all-to-all-start.3) | async-done | bytes 1572896 | tf_op jit(solution)/shard_map/all_to_all | solution.py:82
  163.4 1.1 copy-done.1
  164.6 4.7 %all-to-all-start.1 = ((bf16[16,48,1024]{2,1,0:T(8,128)(2,1)}), bf16[16,48,1024]{2,1,0:T(8,128)(2,1)S(1)}, u32[]{:S(2)}, u32[]{:S(2)}) async-start(bf16[16,48,1024]{2,1,0:T(8,128)(2,1)} %copy.24), calls=%async_computation.1 | async-start | bytes 3145728 | tf_op jit(solution)/shard_map/all_to_all | solution.py:69
  169.3 5.0 %gather_fusion.1 = bf16[384,1024]{1,0:T(8,128)(2,1)} fusion(bf16[768,1024]{1,0:T(8,128)(2,1)} %bitcast.66, s32[1024]{0:T(1024)S(1)} %pad_clamp_fusion), kind=kCustom, calls=%fused_computation.1 | custom fusion | bytes 1574400 | tf_op jit(solution)/shard_map/gather | solution.py:96
  174.3 14.0 %all-to-all-done.1 = bf16[16,48,1024]{2,1,0:T(8,128)(2,1)S(1)} async-done(((bf16[16,48,1024]{2,1,0:T(8,128)(2,1)}), bf16[16,48,1024]{2,1,0:T(8,128)(2,1)S(1)}, u32[]{:S(2)}, u32[]{:S(2)}) %all-to-all-start.1) | async-done | bytes 1572896 | tf_op jit(solution)/shard_map/all_to_all | solution.py:69
  188.2 14.7 %all-to-all-start.4 = ((bf16[8,48,1024]{2,1,0:T(8,128)(2,1)}), bf16[8,48,1024]{2,1,0:T(8,128)(2,1)S(1)}, u32[]{:S(2)}, u32[]{:S(2)}) async-start(bf16[8,48,1024]{2,1,0:T(8,128)(2,1)} %bitcast.76), calls=%async_computation.5 | async-start | bytes 1572864 | tf_op jit(solution)/shard_map/all_to_all | solution.py:97
  202.9 3.5 %bitcast_multiply_fusion = f32[8,64,1024]{2,1,0:T(8,128)} fusion(bf16[16,8,6,64]{3,0,2,1:T(8,128)(2,1)} %get-tuple-element.4, bf16[16,8,6,1024]{3,0,2,1:T(8,128)(2,1)} %bitcast.73), kind=kOutput, calls=%fused_computation.7 | convolution fusion | flops 101187584 | bytes 3768320 | tf_op jit(solution)/shard_map/sacr,sacd->ard/dot_general | solution.py:90
  206.4 1.8 bitcast_multiply_fusion.1
  208.2 2.7 %gather_fusion = bf16[384,1024]{1,0:T(8,128)(2,1)} fusion(bf16[768,1024]{1,0:T(8,128)(2,1)S(1)} %bitcast.65, s32[1024]{0:T(1024)S(1)} %pad_clamp_fusion), kind=kCustom, calls=%fused_computation | custom fusion | bytes 1574400 | tf_op jit(solution)/shard_map/gather | solution.py:89
  210.9 8.9 %all-to-all-done.4 = bf16[8,48,1024]{2,1,0:T(8,128)(2,1)S(1)} async-done(((bf16[8,48,1024]{2,1,0:T(8,128)(2,1)}), bf16[8,48,1024]{2,1,0:T(8,128)(2,1)S(1)}, u32[]{:S(2)}, u32[]{:S(2)}) %all-to-all-start.4) | async-done | bytes 786464 | tf_op jit(solution)/shard_map/all_to_all | solution.py:97
  219.8 0.2 convert_bitcast_fusion
  219.9 0.2 copy.32
  220.1 0.0 all-gather.2.cloned.1.call-done
  220.1 0.9 copy-done.6
  221.1 13.0 %add_convert_fusion.1 = bf16[384,1024]{1,0:T(8,128)(2,1)} fusion(bf16[384,1024]{1,0:T(8,128)(2,1)S(1)} %copy-done.6, bf16[384,8192]{1,0:T(8,128)(2,1)} %all-gather.2.cloned.1.call-done, bf16[8192,1024]{1,0:T(8,128)(2,1)} %param.11), kind=kOutput, calls=%fused_computation.11 | convolution fusion | flops 6443630592 | bytes 24641536 | tf_op jit(solution)/shard_map/dot_general | solution.py:31
  234.1 2.1 add_convert_fusion
  (20 shorter events, 0.1 us)
Async XLA Ops:
  7.2 42.1 %copy-start = (bf16[8,64,1024]{2,1,0:T(8,128)(2,1)S(1)}, bf16[8,64,1024]{2,1,0:T(8,128)(2,1)}, u32[]{:S(2)}) copy-start(bf16[8,64,1024]{2,1,0:T(8,128)(2,1)} %param.12) | copy-start | bytes 3145732
  13.5 28.2 %all-to-all-start = ((bf16[16,48,1024]{2,1,0:T(8,128)(2,1)}), bf16[16,48,1024]{2,1,0:T(8,128)(2,1)S(1)}, u32[]{:S(2)}, u32[]{:S(2)}) async-start(bf16[16,48,1024]{2,1,0:T(8,128)(2,1)} %bitcast.69), calls=%async_computation | async-start | bytes 3145728 | tf_op jit(solution)/shard_map/all_to_all | solution.py:39
  41.8 25.2 %all-to-all-start.2 = ((bf16[16,48,1024]{2,1,0:T(8,128)(2,1)}), bf16[16,48,1024]{2,1,0:T(8,128)(2,1)}, u32[]{:S(2)}, u32[]{:S(2)}) async-start(bf16[16,48,1024]{2,1,0:T(8,128)(2,1)} %bitcast.67), calls=%async_computation.3 | async-start | bytes 3145728 | tf_op jit(solution)/shard_map/all_to_all | solution.py:40
  47.1 86.3 %all-reduce.3.cloned.1.call-start = ((), (), s32[]{:S(2)}) async-start(), calls=%async_computation.8 | async-start | bytes 786432 | tf_op jit(solution)/shard_map/psum | solution.py:55
  48.1 1.2 copy-start.2
  50.5 19.9 %copy-start.5 = (bf16[8,64,1024]{2,1,0:T(8,128)(2,1)S(1)}, bf16[8,64,1024]{2,1,0:T(8,128)(2,1)}, u32[]{:S(2)}) copy-start(bf16[8,64,1024]{2,1,0:T(8,128)(2,1)} %param.13) | copy-start | bytes 3145732
  69.3 1.2 copy-start.4
  71.7 148.4 %all-gather.2.cloned.1.call-start = ((), (), s32[]{:S(2)}) async-start(), calls=%async_computation.6 | async-start | bytes 7077888 | tf_op jit(solution)/shard_map/all_gather | solution.py:32
  72.5 161.7 %reduce-scatter.2.cloned.1.call-start = ((), (), s32[]{:S(2)}) async-start(), calls=%async_computation.7 | async-start | bytes 7077888 | tf_op jit(solution)/shard_map/reduce_scatter | solution.py:100
  136.9 6.7 %copy-start.8 = (bf16[16,8,6,64]{3,0,2,1:T(8,128)(2,1)S(1)}, bf16[16,8,6,64]{3,0,2,1:T(8,128)(2,1)}, u32[]{:S(2)}) copy-start(bf16[16,8,6,64]{3,0,2,1:T(8,128)(2,1)} %get-tuple-element.4) | copy-start | bytes 294916
  136.9 26.5 %all-to-all-start.3 = ((bf16[16,48,1024]{2,1,0:T(8,128)(2,1)}), bf16[16,48,1024]{2,1,0:T(8,128)(2,1)S(1)}, u32[]{:S(2)}, u32[]{:S(2)}) async-start(bf16[16,48,1024]{2,1,0:T(8,128)(2,1)} %copy.26), calls=%async_computation.4 | async-start | bytes 3145728 | tf_op jit(solution)/shard_map/all_to_all | solution.py:82
  163.4 1.1 copy-start.1
  164.6 23.6 %all-to-all-start.1 = ((bf16[16,48,1024]{2,1,0:T(8,128)(2,1)}), bf16[16,48,1024]{2,1,0:T(8,128)(2,1)S(1)}, u32[]{:S(2)}, u32[]{:S(2)}) async-start(bf16[16,48,1024]{2,1,0:T(8,128)(2,1)} %copy.24), calls=%async_computation.1 | async-start | bytes 3145728 | tf_op jit(solution)/shard_map/all_to_all | solution.py:69
  188.2 31.5 %all-to-all-start.4 = ((bf16[8,48,1024]{2,1,0:T(8,128)(2,1)}), bf16[8,48,1024]{2,1,0:T(8,128)(2,1)S(1)}, u32[]{:S(2)}, u32[]{:S(2)}) async-start(bf16[8,48,1024]{2,1,0:T(8,128)(2,1)} %bitcast.76), calls=%async_computation.5 | async-start | bytes 1572864 | tf_op jit(solution)/shard_map/all_to_all | solution.py:97
  202.9 3.5 %copy-start.3 = (bf16[16,48,1024]{2,0,1:T(8,128)(2,1)S(1)}, bf16[16,48,1024]{2,0,1:T(8,128)(2,1)}, u32[]{:S(2)}) copy-start(bf16[16,48,1024]{2,0,1:T(8,128)(2,1)} %copy-done.2) | copy-start | bytes 4718596
  202.9 3.5 %copy-start.7 = (bf16[16,8,6,64]{3,0,2,1:T(8,128)(2,1)S(1)}, bf16[16,8,6,64]{3,0,2,1:T(8,128)(2,1)}, u32[]{:S(2)}) copy-start(bf16[16,8,6,64]{3,0,2,1:T(8,128)(2,1)} %get-tuple-element.5) | copy-start | bytes 294916
  219.9 1.1 copy-start.6
Sparse Core Ops, SparseCore 0:
  71.8 61.5 all-reduce.2
  135.2 42.6 all-gather.1
  180.4 49.8 reduce-scatter.1
where the time goes:
time: 244 us; the launch traced here: 243 us
  waiting for transfers between devices  121 us (50%)
  starting transfers between devices  39.3 us (16%)
  matrix products  36.3 us (15%)
  local copies, waits for them, and re-layouts  27.5 us (11%)
  between operations  13.9 us (6%)
  other arithmetic  4.53 us (2%)
    psum x1, waiting for transfers between devices, local(): lax.psum(down_projection_piece.reshape(flat_shape).astype(jnp.bfloat16),...  48.5 us
    all_to_all x1, waiting for transfers between devices, local(): lax.all_to_all(send_x, 'dp', split_axis=0, concat_axis=0, tiled=True)  16.7 us
    all_to_all x1, waiting for transfers between devices, local(): lax.all_to_all(send_g, 'dp', split_axis=0, concat_axis=0, tiled=True)  16.5 us
    all_to_all x1, waiting for transfers between devices, local(): lax.all_to_all(adapter_backward.astype(jnp.bfloat16).reshape(-1, column_v...  16.1 us
    all_to_all x1, starting transfers between devices, local(): lax.all_to_all(adapter_row_values, 'mp', split_axis=0, concat_axis=1, til...  14.7 us
    all_to_all x1, waiting for transfers between devices, local(): lax.all_to_all(adapter_output.astype(jnp.bfloat16).reshape(-1, column_val...  14 us
    dot_general x1, matrix products, local(): jnp.dot(lax.all_gather(tokens, 'mp', axis=1, tiled=True), frozen_weight_m...  13 us
    dot_general x1, matrix products, local(): lax.dot_general(cotangent, frozen_weight_matrix, (((1,), (1,)), ((), ()))...  12.2 us
  transfers between devices with their start and end apart: 8, of which 6 were waited for; matrix products, arithmetic and copies ran while one was open for 21% of the time, Pallas kernels for 0%

commit v1 on v0

v1 whole, which is shorter than its diff:
```python
import jax
import jax.numpy as jnp
from jax import lax
from jax.experimental import pallas as pl
from jax.experimental.pallas import tpu as pltpu
from jax.sharding import PartitionSpec as P

adapter_scale = 2.0
MESH = pl.DeviceIdType.MESH
bf16, f32, i32 = jnp.bfloat16, jnp.float32, jnp.int32

OFFSETS = (
    (1, 0), (3, 0), (0, 1), (0, 3), (2, 2), (1, 1), (3, 3), (1, 3),
    (3, 1), (2, 0), (0, 2), (2, 1), (1, 2), (2, 3), (3, 2),
)
NT = (((1,), (1,)), ((), ()))
TN = (((0,), (0,)), ((), ()))


def dot(a, b, dims=(((1,), (0,)), ((), ()))):
    return lax.dot_general(a, b, dims, preferred_element_type=f32)


def kernel(
    idx_ref, row_ref, tok_hbm, cot_hbm, w_hbm, a_hbm, b_hbm,
    out_hbm, ig_hbm, da_hbm, db_hbm,
    wv, xall, cot, av, bv, pt, pm, sendg, sendx, recvg, recvx, retb, reto,
    part, pr, r1, r2m, r2p, lbs, lbr, vsg, vrg, fing, vsx, vrx, finx, dg, dx, acc,
    grad, outb, igb,
    wsem, lsem, osem, ag_s, ag_r, g_s, g_r, x_s, x_r, rb_s, rb_r, ro_s, ro_r,
    p_s, p_r, z_s, z_r, agr_s, agr_r, axr_s, axr_r, lb_s, lb_r,
):
    s, m = lax.axis_index("dp"), lax.axis_index("mp")
    x, y, z, c = s // 4, s % 4, m // 2, m % 2
    tok_rows = cot.shape[0]
    slots = pt.shape[1]

    def zdev(step, core_step=0):
        return {"dp": s, "mp": (z + step) % 4 * 2 + (c + core_step) % 2}

    def mp_dev(k):
        return {"dp": s, "mp": (m + k) % 8}

    def dp_at(k):
        return (x + OFFSETS[k][0]) % 4 * 4 + (y + OFFSETS[k][1]) % 4

    def remote(src, dst, send_sem, recv_sem, device):
        return pltpu.make_async_remote_copy(
            src_ref=src, dst_ref=dst, send_sem=send_sem, recv_sem=recv_sem,
            device_id=device, device_id_type=MESH,
        )

    def exchange(send, recv, ss, rs):
        return [
            remote(send.at[dp_at(k)], recv.at[s], ss.at[k], rs.at[k], {"dp": dp_at(k), "mp": m})
            for k in range(15)
        ]

    tok_in = pltpu.make_async_copy(tok_hbm, xall.at[m], lsem.at[0])
    cot_in = pltpu.make_async_copy(cot_hbm, cot, lsem.at[1])
    a_in = pltpu.make_async_copy(a_hbm, av, lsem.at[2])
    b_in = pltpu.make_async_copy(b_hbm, bv, lsem.at[3])

    def w_in(j):
        return pltpu.make_async_copy(w_hbm.at[j], wv.at[j], wsem.at[j])

    barrier = pltpu.get_barrier_semaphore()
    for k in range(15):
        pl.semaphore_signal(barrier, inc=1, device_id={"dp": dp_at(k), "mp": m}, device_id_type=MESH)
    for k in range(1, 8):
        pl.semaphore_signal(barrier, inc=1, device_id=mp_dev(k), device_id_type=MESH)
    tok_in.start()
    cot_in.start()
    b_in.start()
    a_in.start()
    for j in range(8):
        w_in(j).start()

    with jax.named_scope("slots"):
        lane = lax.broadcasted_iota(i32, (tok_rows, 128), 1)
        ids = idx_ref[...]
        storage = jnp.sum(
            jnp.where(lane == ids, row_ref[...].astype(f32), 0.0), axis=1, keepdims=True
        )
        hit = (lane.astype(f32) == storage).astype(f32)
        rr = lax.broadcasted_iota(i32, (tok_rows, tok_rows), 0)
        cc = lax.broadcasted_iota(i32, (tok_rows, tok_rows), 1)
        before = dot((cc < rr).astype(f32).astype(bf16), hit.astype(bf16))
        capacity = slots // 128
        dest = storage * capacity + jnp.sum(before * hit, axis=1, keepdims=True)
        dest_row = jnp.sum(jnp.where(rr == cc, dest, 0.0), axis=0, keepdims=True)
        wide = lax.broadcasted_iota(i32, (tok_rows, slots), 1).astype(f32)
        pt[...] = (wide == dest).astype(f32).astype(bf16)
        tall = lax.broadcasted_iota(i32, (slots, tok_rows), 0).astype(f32)
        pm[...] = (tall == dest_row).astype(f32).astype(bf16)

    def place(src, dst):
        def body(i, carry):
            cols = pl.ds(pl.multiple_of(i * 256, 256), 256)
            dst[:, :, cols] = dot(pm[...], src[:, cols]).astype(bf16).reshape(16, 48, 256)
            return carry

        lax.fori_loop(0, 4, body, 0)

    with jax.named_scope("barrier"):
        tok_in.wait()
        pl.semaphore_wait(barrier, 22)

    mine = xall.at[m]
    ag = [
        remote(mine, mine, ag_s.at[0], ag_r.at[0], zdev(1)),
        remote(mine, mine, ag_s.at[1], ag_r.at[1], zdev(3)),
        remote(mine, mine, ag_s.at[2], ag_r.at[2], zdev(0, 1)),
    ]
    for copy in ag:
        copy.start()

    cot_in.wait()
    with jax.named_scope("place_cot"):
        place(cot, sendg)
    g_x = exchange(sendg, recvg, g_s, g_r)
    for copy in g_x:
        copy.start()
    recvg[s] = sendg[s]
    with jax.named_scope("place_tok"):
        place(xall.at[m], sendx)
    recvx[s] = sendx[s]

    def pair(j):
        return remote(part.at[j, :, 1 - c], pr.at[j], p_s.at[j], p_r.at[j], zdev(0, 1))

    def frozen_back(j, carry):
        w_in(j).wait()

        def tile(i, inner):
            cols = pl.ds(pl.multiple_of(i * 256, 256), 256)
            v = dot(cot[...], wv[j, cols, :], NT)
            part[j, :, :, :, cols] = v.astype(bf16).reshape(4, 2, 48, 256)
            return inner

        lax.fori_loop(0, 4, tile, 0)
        pair(j).start()
        return carry

    with jax.named_scope("frozen_back"):
        lax.fori_loop(0, 8, frozen_back, 0)

    x_x = exchange(sendx, recvx, x_s, x_r)
    with jax.named_scope("start_x"):
        for k in range(15):
            g_x[k].wait_send()
            x_x[k].start()

    below, above, far = (z + 3) % 4, (z + 1) % 4, (z + 2) % 4
    lo_rows, hi_rows = pl.ds(0, tok_rows // 2), pl.ds(tok_rows // 2, tok_rows // 2)
    with jax.named_scope("tokens_forward"):
        ag[0].wait_recv()
        from_below, from_above = xall.at[below * 2 + c], xall.at[above * 2 + c]
        far_lo, far_hi = xall.at[far * 2 + c, lo_rows], xall.at[far * 2 + c, hi_rows]
        ag2 = [
            remote(from_below.at[lo_rows], from_below.at[lo_rows], ag_s.at[3], ag_r.at[3], zdev(1)),
            remote(from_above.at[hi_rows], from_above.at[hi_rows], ag_s.at[4], ag_r.at[4], zdev(3)),
            remote(from_below, from_below, ag_s.at[5], ag_r.at[5], zdev(0, 1)),
            remote(from_above, from_above, ag_s.at[6], ag_r.at[6], zdev(0, 1)),
            remote(far_lo, far_lo, ag_s.at[7], ag_r.at[7], zdev(0, 1)),
            remote(far_hi, far_hi, ag_s.at[8], ag_r.at[8], zdev(0, 1)),
        ]
        ag2[0].start()
        ag2[2].start()
        ag[1].wait_recv()
        ag2[1].start()
        ag2[3].start()

    row48 = lax.broadcasted_iota(i32, (48, 512), 0)
    first = (lax.broadcasted_iota(i32, (48, 512), 1) >> 6) * capacity
    keep = ((row48 >= first) & (row48 < first + capacity))[None]

    def project(recv, factor, vs):
        total = None
        for h in range(2):
            v = dot(recv[pl.ds(8 * h, 8)].reshape(384, 1024), factor[...], NT)
            v = jnp.where(keep, v.reshape(8, 48, 512), 0.0).astype(bf16).reshape(384, 512)
            r = lax.broadcasted_iota(i32, (512, 128), 0) & 63
            q = lax.broadcasted_iota(i32, (512, 128), 1)
            v = dot(v, (q == r + 64 * h).astype(f32).astype(bf16))
            total = v if total is None else total + v
        vs[...] = total.astype(bf16).reshape(8, 48, 128)

    def spread(fin, d):
        for h in range(2):
            q = lax.broadcasted_iota(i32, (128, 512), 0)
            r = lax.broadcasted_iota(i32, (128, 512), 1) & 63
            v = dot(fin[...].reshape(384, 128), (q == r + 64 * h).astype(f32).astype(bf16))
            v = jnp.where(keep, v.reshape(8, 48, 512), 0.0).astype(bf16)
            d[pl.ds(h * 384, 384), :] = v.reshape(384, 512)

    def rank_scatter(vs, vr, ss, rs):
        return [
            remote(vs.at[(m + k) % 8], vr.at[m], ss.at[k - 1], rs.at[k - 1], mp_dev(k))
            for k in range(1, 8)
        ]

    def rank_gather(fin, ss, rs):
        return [
            remote(fin.at[m], fin.at[m], ss.at[k + 6], rs.at[k + 6], mp_dev(k)) for k in range(1, 8)
        ]

    def rank_sum(vs, vr, fin):
        vr[m] = vs[m]
        fin[m] = jnp.sum(vr[...].astype(f32), axis=0).astype(bf16)

    b_in.wait()
    with jax.named_scope("wait_g"):
        for copy in g_x:
            copy.wait_recv()
    with jax.named_scope("project_g"):
        project(recvg, bv, vsg)
    g1 = rank_scatter(vsg, vrg, agr_s, agr_r)
    for copy in g1:
        copy.start()

    def pair_sum(j, carry):
        pair(j).wait_recv()
        for q in range(4):
            part[j, q, c] = (part[j, q, c].astype(f32) + pr[j, q].astype(f32)).astype(bf16)
        return carry

    with jax.named_scope("pair_sum"):
        lax.fori_loop(0, 8, pair_sum, 0)
    lo, hi = pl.ds(0, 4), pl.ds(4, 4)
    zc = [
        remote(part.at[lo, far, c], r1.at[lo], z_s.at[0], z_r.at[0], zdev(1)),
        remote(part.at[hi, far, c], r1.at[hi], z_s.at[1], z_r.at[1], zdev(3)),
        remote(part.at[hi, above, c], r2m.at[hi], z_s.at[2], z_r.at[2], zdev(1)),
        remote(part.at[lo, below, c], r2p.at[lo], z_s.at[3], z_r.at[3], zdev(3)),
        remote(part.at[lo, above, c], r2m.at[lo], z_s.at[4], z_r.at[4], zdev(1)),
        remote(part.at[hi, below, c], r2p.at[hi], z_s.at[5], z_r.at[5], zdev(3)),
    ]
    for copy in zc[:4]:
        copy.start()

    with jax.named_scope("rank_sum_g"):
        for copy in g1:
            copy.wait_recv()
        rank_sum(vsg, vrg, fing)
    g2 = rank_gather(fing, agr_s, agr_r)
    for copy in g2:
        copy.start()

    def forward(slot, start):
        def tile(i, carry):
            cols = pl.ds(pl.multiple_of(i * 256, 256), 256)
            v = dot(xall[slot], wv[slot, :, cols])
            acc[:, cols] = v if start else acc[:, cols] + v
            return carry

        lax.fori_loop(0, 4, tile, 0)

    with jax.named_scope("forward_own"):
        forward(m, True)
        ag[2].wait_recv()
        forward(m + 1 - 2 * c, False)

    a_in.wait()
    with jax.named_scope("wait_rank_g"):
        for copy in g2:
            copy.wait_recv()

    def lora(d, factor, send):
        def tile(i, carry):
            cols = pl.ds(pl.multiple_of(i * 256, 256), 256)
            v = adapter_scale * dot(d[...], factor[:, cols])
            send[:, :, cols] = v.astype(bf16).reshape(16, 48, 256)
            return carry

        lax.fori_loop(0, 4, tile, 0)

    with jax.named_scope("lora_back"):
        spread(fing, dg)
        lora(dg, av, sendg)
    rb = exchange(sendg, retb, rb_s, rb_r)
    with jax.named_scope("start_rb"):
        for k in range(15):
            x_x[k].wait_send()
            rb[k].start()
    retb[s] = sendg[s]

    with jax.named_scope("tokens_far"):
        ag2[0].wait_recv()
        ag2[4].start()
        ag2[1].wait_recv()
        ag2[5].start()

    with jax.named_scope("wait_x"):
        for copy in x_x:
            copy.wait_recv()
    with jax.named_scope("project_x"):
        project(recvx, av, vsx)
    x1 = rank_scatter(vsx, vrx, axr_s, axr_r)
    for copy in x1:
        copy.start()

    with jax.named_scope("ring_second"):
        zc[0].wait_recv()

        def add_lo(j, carry):
            part[j, above, c] = (part[j, above, c].astype(f32) + r1[j].astype(f32)).astype(bf16)
            return carry

        lax.fori_loop(0, 4, add_lo, 0)
        zc[4].start()
        zc[1].wait_recv()

        def add_hi(j, carry):
            part[j, below, c] = (part[j, below, c].astype(f32) + r1[j].astype(f32)).astype(bf16)
            return carry

        lax.fori_loop(4, 8, add_hi, 0)
        zc[5].start()

    with jax.named_scope("rank_sum_x"):
        for copy in x1:
            copy.wait_recv()
        rank_sum(vsx, vrx, finx)
    x2 = rank_gather(finx, axr_s, axr_r)
    for copy in x2:
        copy.start()

    def factor_gradient(d, recv):
        def tile(i, carry):
            cols = pl.ds(pl.multiple_of(i * 256, 256), 256)
            v = dot(d[...], recv[:, :, cols].reshape(768, 256), TN)
            grad[:, cols] = adapter_scale * v
            return carry

        lax.fori_loop(0, 4, tile, 0)

    with jax.named_scope("first_gradient"):
        factor_gradient(dg, recvx)
    da_out = pltpu.make_async_copy(grad, da_hbm, osem.at[0])
    da_out.start()

    with jax.named_scope("wait_rank_x"):
        for copy in x2:
            copy.wait_recv()
    with jax.named_scope("lora_out"):
        spread(finx, dx)
        lora(dx, bv, sendx)
    ro = exchange(sendx, reto, ro_s, ro_r)
    with jax.named_scope("start_ro"):
        for k in range(15):
            rb[k].wait_send()
            ro[k].start()
    reto[s] = sendx[s]

    with jax.named_scope("second_gradient"):
        da_out.wait()
        factor_gradient(dx, recvg)
    db_out = pltpu.make_async_copy(grad, db_hbm, osem.at[1])
    db_out.start()

    with jax.named_scope("forward_rest"):
        ag2[2].wait_recv()
        ag2[3].wait_recv()
        ag2[4].wait_recv()
        ag2[5].wait_recv()

        def rest(k, carry):
            forward((m // 2 * 2 + 2 + k) % 8, False)
            return carry

        lax.fori_loop(0, 6, rest, 0)

    with jax.named_scope("wait_rb"):
        for copy in rb:
            copy.wait_recv()

    with jax.named_scope("pick_back"):

        def pick(i, carry):
            cols = pl.ds(pl.multiple_of(i * 256, 256), 256)
            v = dot(pt[...], retb[:, :, cols].reshape(768, 256))
            lbs[:, :, cols] = v.astype(bf16).reshape(8, 48, 256)
            return carry

        lax.fori_loop(0, 4, pick, 0)
    lb = [
        remote(lbs.at[(m + k) % 8], lbr.at[m], lb_s.at[k - 1], lb_r.at[k - 1], mp_dev(k))
        for k in range(1, 8)
    ]
    for copy in lb:
        copy.start()
    lbr[m] = lbs[m]

    with jax.named_scope("wait_ring"):
        for copy in zc[2:]:
            copy.wait_recv()
    with jax.named_scope("wait_lb"):
        for copy in lb:
            copy.wait_recv()

    with jax.named_scope("input_gradient"):
        for j in range(8):
            v = part[j, z, c].astype(f32) + r2m[j].astype(f32) + r2p[j].astype(f32)
            igb[:, j * 1024 : (j + 1) * 1024] = (v + lbr[j].astype(f32)).astype(bf16)
    ig_out = pltpu.make_async_copy(igb, ig_hbm, osem.at[2])
    ig_out.start()

    with jax.named_scope("wait_ro"):
        for copy in ro:
            copy.wait_recv()
    with jax.named_scope("output"):

        def finish(i, carry):
            cols = pl.ds(pl.multiple_of(i * 256, 256), 256)
            v = dot(pt[...], reto[:, :, cols].reshape(768, 256))
            outb[:, cols] = (acc[:, cols] + v).astype(bf16)
            return carry

        lax.fori_loop(0, 4, finish, 0)
    out_out = pltpu.make_async_copy(outb, out_hbm, osem.at[3])
    out_out.start()

    with jax.named_scope("drain"):
        for copy in ag + ag2 + ro + zc + g1 + g2 + x1 + x2 + lb:
            copy.wait_send()

        def drain(j, carry):
            pair(j).wait_send()
            return carry

        lax.fori_loop(0, 8, drain, 0)
        db_out.wait()
        ig_out.wait()
        out_out.wait()


def local(tokens, cotangent, index, storage_row, weight, first_factors, second_factors):
    tok_rows, cols = tokens.shape
    residents, rank, _ = first_factors.shape
    adapters = storage_row.shape[0]
    slots = adapters * max(2, 2 * tok_rows // adapters)
    per = slots // 16
    own = tok_rows // 8
    wide = residents * rank
    anywhere = pl.BlockSpec(memory_space=pl.ANY)
    vmem = pl.BlockSpec(memory_space=pltpu.VMEM)
    dma = pltpu.SemaphoreType.DMA
    rows = pltpu.VMEM((16, per, cols), bf16)
    blocks = pltpu.VMEM((8, own, cols), bf16)
    ranks = pltpu.VMEM((8, own, 128), bf16)
    output, input_gradient, first_gradient, second_gradient = pl.pallas_call(
        kernel,
        out_shape=(
            jax.ShapeDtypeStruct((tok_rows, cols), bf16),
            jax.ShapeDtypeStruct((own, 8 * cols), bf16),
            jax.ShapeDtypeStruct((wide, cols), f32),
            jax.ShapeDtypeStruct((wide, cols), f32),
        ),
        in_specs=[vmem, vmem] + [anywhere] * 5,
        out_specs=[anywhere] * 4,
        scratch_shapes=[
            pltpu.VMEM((8, cols, cols), bf16),
            pltpu.VMEM((8, tok_rows, cols), bf16),
            pltpu.VMEM((tok_rows, cols), bf16),
            pltpu.VMEM((wide, cols), bf16),
            pltpu.VMEM((wide, cols), bf16),
            pltpu.VMEM((tok_rows, slots), bf16),
            pltpu.VMEM((slots, tok_rows), bf16),
            rows, rows, rows, rows, rows, rows,
            pltpu.VMEM((8, 4, 2, own, cols), bf16),
            pltpu.VMEM((8, 4, own, cols), bf16),
            blocks, blocks, blocks, blocks, blocks,
            ranks, ranks, ranks, ranks, ranks, ranks,
            pltpu.VMEM((slots, wide), bf16),
            pltpu.VMEM((slots, wide), bf16),
            pltpu.VMEM((tok_rows, cols), f32),
            pltpu.VMEM((wide, cols), f32),
            pltpu.VMEM((tok_rows, cols), bf16),
            pltpu.VMEM((own, 8 * cols), bf16),
            dma((8,)), dma((4,)), dma((4,)),
            dma((9,)), dma((9,)),
            dma((15,)), dma((15,)), dma((15,)), dma((15,)),
            dma((15,)), dma((15,)), dma((15,)), dma((15,)),
            dma((8,)), dma((8,)), dma((6,)), dma((6,)),
            dma((14,)), dma((14,)), dma((14,)), dma((14,)),
            dma((7,)), dma((7,)),
        ],
        compiler_params=pltpu.CompilerParams(
            collective_id=0, has_side_effects=True, vmem_limit_bytes=62 * 2**20
        ),
        cost_estimate=pl.CostEstimate(
            flops=20_000_000_000, bytes_accessed=30_000_000, transcendentals=0
        ),
        name="adapter_step",
    )(
        index,
        storage_row.reshape(1, adapters),
        tokens,
        cotangent,
        weight.reshape(8, cols, cols),
        first_factors.reshape(wide, cols),
        second_factors.reshape(wide, cols),
    )
    shape = first_factors.shape
    return output, input_gradient, first_gradient.reshape(shape), second_gradient.reshape(shape)


def solution(mesh):
    in_specs = (
        P("dp", "mp"),
        P("dp", "mp"),
        P("dp", None),
        P(),
        P(None, "mp"),
        P("dp", None, "mp"),
        P("dp", None, "mp"),
    )
    out_specs = (P("dp", "mp"), P(("dp", "mp"), None), P("dp", None, "mp"), P("dp", None, "mp"))
    return jax.shard_map(local, mesh=mesh, in_specs=in_specs, out_specs=out_specs, check_vma=False)
```

time: 244 us -> 116 us (0.48)
  waiting for transfers between devices: 121 us -> 0 us
  Pallas kernels: 0 us -> 105 us
  starting transfers between devices: 39.3 us -> 0 us
  matrix products: 36.3 us -> 0 us
  local copies, waits for them, and re-layouts: 27.5 us -> 9.44 us
  between operations: 13.9 us -> 0.65 us
  other arithmetic: 4.53 us -> 0 us
    pallas_call x0 -> x1, Pallas kernels: none -> 105 us  [local(): pl.pallas_call(kernel, out_shape=(jax.ShapeDtypeStruct((tok_rows, cols),...]
    all_to_all x5 -> x0, waiting for transfers between devices: 72.1 us -> none  [the longest x1 16.7 us: local(): lax.all_to_all(send_x, 'dp', split_axis=0, concat_axis=0, tiled=True)]
    psum x1 -> x0, waiting for transfers between devices: 48.5 us -> none  [local(): lax.psum(down_projection_piece.reshape(flat_shape).astype(jnp.bfloat16),...]
    all_to_all x5 -> x0, starting transfers between devices: 39 us -> none  [the longest x1 14.7 us: local(): lax.all_to_all(adapter_row_values, 'mp', split_axis=0, concat_axis=1, til...]
    dot_general x8 -> x0, matrix products: 36.3 us -> none  [the longest x1 13 us: local(): jnp.dot(lax.all_gather(tokens, 'mp', axis=1, tiled=True), frozen_weight_m...]
    scatter x2 -> x0, local copies, waits for them, and re-layouts: 7.94 us -> none  [the longest x1 3.97 us: local(): send_x = blank.at[destination].set(tokens)]
    gather x2 -> x0, local copies, waits for them, and re-layouts: 7.67 us -> none  [the longest x1 4.99 us: local(): adapter_row_values = backward_returned[destination]]
    all_to_all x4 -> x0, local copies, waits for them, and re-layouts: 7.16 us -> none  [the longest x1 2.27 us: local(): lax.all_to_all(send_g, 'dp', split_axis=0, concat_axis=0, tiled=True)]
  transfers between devices with their start and end apart: 8 -> 0, of which waited for: 6 -> 0; matrix products, arithmetic and copies ran while one was open for 21% -> 0% of each run, Pallas kernels for 0% -> 0%
where the time goes in v1:
time: 116 us
  Pallas kernels  105 us (91%)
  local copies, waits for them, and re-layouts  9.44 us (8%)
    pallas_call x1, Pallas kernels, local(): pl.pallas_call(kernel, out_shape=(jax.ShapeDtypeStruct((tok_rows, cols),...  105 us
    unnamed x9, local copies, waits for them, and re-layouts  9.44 us

profile of v1, /device:TPU:1, one launch (start us, length us, event | category | flops | bytes accessed | tf_op | source)
XLA Modules:
  0.0 115.5 jit_solution(14224201602684223200)
XLA Ops:
  0.6 1.5 %copy.11.idx_ref = s32[384,1]{1,0:T(8,128)} copy(s32[384,1]{0,1:T(1,128)} %param.9) | data formatting | bytes 3072 | tf_op args[2]
  2.1 105.4 %adapter_step.1 = (bf16[384,1024]{1,0:T(8,128)(2,1)}, bf16[48,8192]{1,0:T(8,128)(2,1)}, f32[512,1024]{1,0:T(8,128)}, f32[512,1024]{1,0:T(8,128)}) custom-call(s32[384,1]{1,0:T(8,128)} %copy.11.idx_ref, s32[1,128]{1,0:T(1,128)} %bitcast.11, bf16[384,1024]{1,0:T(8,128)(2,1)} %tok_hbm.1, bf16[384,1024]{1,0:T(8,128)(2,1)} %cot_hbm.1, ...), custom_call_target="tpu_custom_call" | custom-call | flops 20000000000 | bytes 30000000 | tf_op jit(solution)/shard_map/adapter_step/pallas_call | solution.py:452
  107.6 0.0 copy-start.1
  107.6 2.2 %copy.16 = bf16[384,1024]{1,0:T(8,128)(2,1)} copy(bf16[384,1024]{1,0:T(8,128)(2,1)} %get-tuple-element.16) | data formatting | bytes 1572864
  109.8 2.1 %copy.17 = bf16[48,8192]{1,0:T(8,128)(2,1)} copy(bf16[48,8192]{1,0:T(8,128)(2,1)} %get-tuple-element.17) | data formatting | bytes 1572864
  111.9 0.0 copy-done.1
  111.9 0.0 copy-start
  111.9 1.3 %copy.18 = f32[8,64,1024]{2,1,0:T(8,128)} copy(f32[8,64,1024]{2,1,0:T(8,128)S(1)} %bitcast.7) | data formatting | bytes 4194304
  113.2 1.0 copy-done
  114.2 1.3 %copy.19 = f32[8,64,1024]{2,1,0:T(8,128)} copy(f32[8,64,1024]{2,1,0:T(8,128)S(1)} %bitcast.6) | data formatting | bytes 4194304
Async XLA Ops:
  107.6 4.3 %copy-start.1 = (f32[512,1024]{1,0:T(8,128)S(1)}, f32[512,1024]{1,0:T(8,128)}, u32[]{:S(2)}) copy-start(f32[512,1024]{1,0:T(8,128)} %get-tuple-element.10) | copy-start | bytes 6291460
  111.9 2.3 %copy-start = (f32[512,1024]{1,0:T(8,128)S(1)}, f32[512,1024]{1,0:T(8,128)}, u32[]{:S(2)}) copy-start(f32[512,1024]{1,0:T(8,128)} %get-tuple-element.11) | copy-start | bytes 6291460

commit v2 on v1

v2 whole, which is shorter than its diff:
```python
import jax
import jax.numpy as jnp
from jax import lax
from jax.experimental import pallas as pl
from jax.experimental.pallas import tpu as pltpu
from jax.sharding import PartitionSpec as P

adapter_scale = 2.0
MESH = pl.DeviceIdType.MESH
bf16, f32, i32 = jnp.bfloat16, jnp.float32, jnp.int32

OFFSETS = (
    (1, 0), (3, 0), (0, 1), (0, 3), (2, 2), (1, 1), (3, 3), (1, 3),
    (3, 1), (2, 0), (0, 2), (2, 1), (1, 2), (2, 3), (3, 2),
)
NT = (((1,), (1,)), ((), ()))
TN = (((0,), (0,)), ((), ()))


def dot(a, b, dims=(((1,), (0,)), ((), ()))):
    return lax.dot_general(a, b, dims, preferred_element_type=f32)


def kernel(
    idx_hbm, row_hbm, tok_hbm, cot_hbm, w_hbm, a_hbm, b_hbm,
    out_hbm, ig_hbm, da_hbm, db_hbm,
    idx_ref, row_ref, wv, xall, cot, av, bv, pt, pm, sendg, sendx, recvg, recvx, retb, reto,
    part, pr, r1, r2m, r2p, lbs, lbr, vsg, vrg, fing, vsx, vrx, finx, dg, dx, acc,
    grad, outb, igb,
    wsem, lsem, osem, ag_s, ag_r, g_s, g_r, x_s, x_r, rb_s, rb_r, ro_s, ro_r,
    p_s, p_r, z_s, z_r, rk_s, rk_r, lb_s, lb_r,
):
    s, m = lax.axis_index("dp"), lax.axis_index("mp")
    x, y, z, c = s // 4, s % 4, m // 2, m % 2
    tok_rows = cot.shape[0]
    slots = pt.shape[1]

    def zdev(step, core_step=0):
        return {"dp": s, "mp": (z + step) % 4 * 2 + (c + core_step) % 2}

    def mp_dev(k):
        return {"dp": s, "mp": (m + k) % 8}

    def dp_at(k):
        return (x + OFFSETS[k][0]) % 4 * 4 + (y + OFFSETS[k][1]) % 4

    def remote(src, dst, send_sem, recv_sem, device):
        return pltpu.make_async_remote_copy(
            src_ref=src, dst_ref=dst, send_sem=send_sem, recv_sem=recv_sem,
            device_id=device, device_id_type=MESH,
        )

    def exchange(send, recv, ss, rs):
        return [
            remote(send.at[dp_at(k)], recv.at[s], ss, rs, {"dp": dp_at(k), "mp": m})
            for k in range(15)
        ]

    def landed(ref, sem):
        pltpu.make_async_copy(ref, ref, sem).wait()

    tok_in = pltpu.make_async_copy(tok_hbm, xall.at[m], lsem.at[0])
    cot_in = pltpu.make_async_copy(cot_hbm, cot, lsem.at[1])
    a_in = pltpu.make_async_copy(a_hbm, av, lsem.at[2])
    idx_in = pltpu.make_async_copy(idx_hbm, idx_ref, lsem.at[4])
    row_in = pltpu.make_async_copy(row_hbm, row_ref, lsem.at[5])
    b_in = pltpu.make_async_copy(b_hbm, bv, lsem.at[3])

    def w_in(j):
        return pltpu.make_async_copy(w_hbm.at[j], wv.at[j], wsem.at[j])

    idx_in.start()
    row_in.start()
    barrier = pltpu.get_barrier_semaphore()
    for k in range(15):
        pl.semaphore_signal(barrier, inc=1, device_id={"dp": dp_at(k), "mp": m}, device_id_type=MESH)
    for k in range(1, 8):
        pl.semaphore_signal(barrier, inc=1, device_id=mp_dev(k), device_id_type=MESH)
    tok_in.start()
    cot_in.start()

    with jax.named_scope("slots"):
        idx_in.wait()
        row_in.wait()
        lane = lax.broadcasted_iota(i32, (tok_rows, 128), 1)
        rr = lax.broadcasted_iota(i32, (tok_rows, tok_rows), 0)
        cc = lax.broadcasted_iota(i32, (tok_rows, tok_rows), 1)
        ids = jnp.sum(
            jnp.where(rr == cc, idx_ref[...].astype(f32), 0.0), axis=1, keepdims=True
        )
        storage = jnp.sum(
            jnp.where(lane.astype(f32) == ids, row_ref[...].astype(f32), 0.0), axis=1, keepdims=True
        )
        hit = (lane.astype(f32) == storage).astype(f32)
        before = dot((cc < rr).astype(f32).astype(bf16), hit.astype(bf16))
        capacity = slots // 128
        dest = storage * capacity + jnp.sum(before * hit, axis=1, keepdims=True)
        dest_row = jnp.sum(jnp.where(rr == cc, dest, 0.0), axis=0, keepdims=True)
        wide = lax.broadcasted_iota(i32, (tok_rows, slots), 1).astype(f32)
        pt[...] = (wide == dest).astype(f32).astype(bf16)
        tall = lax.broadcasted_iota(i32, (slots, tok_rows), 0).astype(f32)
        pm[...] = (tall == dest_row).astype(f32).astype(bf16)

    def place(src, dst):
        def body(i, carry):
            cols = pl.ds(pl.multiple_of(i * 256, 256), 256)
            dst[:, :, cols] = dot(pm[...], src[:, cols]).astype(bf16).reshape(16, 48, 256)
            return carry

        lax.fori_loop(0, 4, body, 0)

    cot_in.wait()
    for j in range(8):
        w_in(j).start()
    b_in.start()
    a_in.start()
    with jax.named_scope("place_cot"):
        place(cot, sendg)
        recvg[s] = sendg[s]
    with jax.named_scope("barrier"):
        tok_in.wait()
        pl.semaphore_wait(barrier, 22)

    mine = xall.at[m]
    ag = [
        remote(mine, mine, ag_s, ag_r.at[0], zdev(1)),
        remote(mine, mine, ag_s, ag_r.at[1], zdev(3)),
        remote(mine, mine, ag_s, ag_r.at[2], zdev(0, 1)),
    ]
    for copy in ag:
        copy.start()


    g_x = exchange(sendg, recvg, g_s, g_r)
    for copy in g_x:
        copy.start()
    with jax.named_scope("place_tok"):
        place(xall.at[m], sendx)
        recvx[s] = sendx[s]

    def pair(j):
        return remote(part.at[j, :, 1 - c], pr.at[j], p_s, p_r, zdev(0, 1))

    def frozen_back(j, carry):
        w_in(j).wait()

        def tile(i, inner):
            cols = pl.ds(pl.multiple_of(i * 256, 256), 256)
            v = dot(cot[...], wv[j, cols, :], NT)
            part[j, :, :, :, cols] = v.astype(bf16).reshape(4, 2, 48, 256)
            return inner

        lax.fori_loop(0, 4, tile, 0)
        pair(j).start()
        return carry

    with jax.named_scope("frozen_back"):
        lax.fori_loop(0, 5, frozen_back, 0)

    x_x = exchange(sendx, recvx, x_s, x_r)
    for copy in x_x:
        copy.start()
    with jax.named_scope("frozen_back_2"):
        lax.fori_loop(5, 8, frozen_back, 0)

    def pair_sum(j, carry):
        for q in range(4):
            part[j, q, c] = (part[j, q, c].astype(f32) + pr[j, q].astype(f32)).astype(bf16)
        return carry

    with jax.named_scope("pair_sum"):
        landed(pr, p_r)
        lax.fori_loop(0, 8, pair_sum, 0)
    def forward(slot, start):
        def tile(i, carry):
            cols = pl.ds(pl.multiple_of(i * 256, 256), 256)
            v = dot(xall[slot], wv[slot, :, cols])
            acc[:, cols] = v if start else acc[:, cols] + v
            return carry

        lax.fori_loop(0, 4, tile, 0)

    with jax.named_scope("forward_own"):
        forward(m, True)
        ag[2].wait_recv()
        forward(m + 1 - 2 * c, False)

    below, above, far = (z + 3) % 4, (z + 1) % 4, (z + 2) % 4
    lo_rows, hi_rows = pl.ds(0, tok_rows // 2), pl.ds(tok_rows // 2, tok_rows // 2)
    row48 = lax.broadcasted_iota(i32, (48, 512), 0)
    first = (lax.broadcasted_iota(i32, (48, 512), 1) >> 6) * capacity
    keep = ((row48 >= first) & (row48 < first + capacity))[None]

    def project(recv, factor, vs):
        total = None
        for h in range(2):
            v = dot(recv[pl.ds(8 * h, 8)].reshape(384, 1024), factor[...], NT)
            v = jnp.where(keep, v.reshape(8, 48, 512), 0.0).astype(bf16).reshape(384, 512)
            r = lax.broadcasted_iota(i32, (512, 128), 0) & 63
            q = lax.broadcasted_iota(i32, (512, 128), 1)
            v = dot(v, (q == r + 64 * h).astype(f32).astype(bf16))
            total = v if total is None else total + v
        vs[...] = total.astype(bf16).reshape(8, 48, 128)

    def spread(fin, d):
        for h in range(2):
            q = lax.broadcasted_iota(i32, (128, 512), 0)
            r = lax.broadcasted_iota(i32, (128, 512), 1) & 63
            v = dot(fin[...].reshape(384, 128), (q == r + 64 * h).astype(f32).astype(bf16))
            v = jnp.where(keep, v.reshape(8, 48, 512), 0.0).astype(bf16)
            d[pl.ds(h * 384, 384), :] = v.reshape(384, 512)

    def rank_scatter(vs, vr, ss, rs):
        return [
            remote(vs.at[(m + k) % 8], vr.at[m], ss, rs, mp_dev(k))
            for k in range(1, 8)
        ]

    def rank_gather(fin, ss, rs):
        return [
            remote(fin.at[m], fin.at[m], ss, rs, mp_dev(k)) for k in range(1, 8)
        ]

    def rank_sum(vs, vr, fin):
        vr[m] = vs[m]
        fin[m] = jnp.sum(vr[...].astype(f32), axis=0).astype(bf16)

    b_in.wait()
    with jax.named_scope("wait_g"):
        landed(recvg.at[pl.ds(0, 15)], g_r)
    with jax.named_scope("project_g"):
        project(recvg, bv, vsg)
    g1 = rank_scatter(vsg, vrg, rk_s, rk_r.at[0])
    for copy in g1:
        copy.start()

    lo, hi = pl.ds(0, 4), pl.ds(4, 4)
    zc = [
        remote(part.at[lo, far, c], r1.at[lo], z_s, z_r.at[0], zdev(1)),
        remote(part.at[hi, far, c], r1.at[hi], z_s, z_r.at[1], zdev(3)),
        remote(part.at[hi, above, c], r2m.at[hi], z_s, z_r.at[2], zdev(1)),
        remote(part.at[lo, below, c], r2p.at[lo], z_s, z_r.at[2], zdev(3)),
        remote(part.at[lo, above, c], r2m.at[lo], z_s, z_r.at[2], zdev(1)),
        remote(part.at[hi, below, c], r2p.at[hi], z_s, z_r.at[2], zdev(3)),
    ]
    with jax.named_scope("tokens_forward"):
        ag[0].wait_recv()
        from_below, from_above = xall.at[below * 2 + c], xall.at[above * 2 + c]
        far_lo, far_hi = xall.at[far * 2 + c, lo_rows], xall.at[far * 2 + c, hi_rows]
        ag2 = [
            remote(from_below.at[lo_rows], from_below.at[lo_rows], ag_s, ag_r.at[3], zdev(1)),
            remote(from_above.at[hi_rows], from_above.at[hi_rows], ag_s, ag_r.at[4], zdev(3)),
            remote(from_below, from_below, ag_s, ag_r.at[5], zdev(0, 1)),
            remote(from_above, from_above, ag_s, ag_r.at[6], zdev(0, 1)),
            remote(far_lo, far_lo, ag_s, ag_r.at[7], zdev(0, 1)),
            remote(far_hi, far_hi, ag_s, ag_r.at[8], zdev(0, 1)),
        ]
        ag2[0].start()
        ag2[2].start()
        ag[1].wait_recv()
        ag2[1].start()
        ag2[3].start()

    with jax.named_scope("rank_sum_g"):
        landed(vrg.at[pl.ds(0, 7)], rk_r.at[0])
        landed(vsg.at[pl.ds(0, 7)], rk_s)
        rank_sum(vsg, vrg, fing)
    g2 = rank_gather(fing, rk_s, rk_r.at[1])
    for copy in g2 + zc[:2]:
        copy.start()

    a_in.wait()
    with jax.named_scope("wait_rank_g"):
        landed(fing.at[pl.ds(0, 7)], rk_r.at[1])
        landed(fing.at[pl.ds(0, 7)], rk_s)

    def lora(d, factor, send):
        def tile(i, carry):
            cols = pl.ds(pl.multiple_of(i * 256, 256), 256)
            v = adapter_scale * dot(d[...], factor[:, cols])
            send[:, :, cols] = v.astype(bf16).reshape(16, 48, 256)
            return carry

        lax.fori_loop(0, 4, tile, 0)

    with jax.named_scope("lora_back"):
        landed(sendg.at[pl.ds(0, 15)], g_s)
        spread(fing, dg)
        lora(dg, av, sendg)
    rb = exchange(sendg, retb, rb_s, rb_r)
    for copy in rb:
        copy.start()
    retb[s] = sendg[s]

    with jax.named_scope("wait_x"):
        landed(recvx.at[pl.ds(0, 15)], x_r)
    with jax.named_scope("project_x"):
        project(recvx, av, vsx)
    x1 = rank_scatter(vsx, vrx, rk_s, rk_r.at[2])
    for copy in x1 + zc[2:4]:
        copy.start()

    with jax.named_scope("tokens_far"):
        ag2[0].wait_recv()
        ag2[4].start()
        ag2[1].wait_recv()
        ag2[5].start()

    with jax.named_scope("forward_below"):
        ag2[2].wait_recv()
        forward(below * 2, False)
        forward(below * 2 + 1, False)

    with jax.named_scope("ring_second"):
        zc[0].wait_recv()

        def add_lo(j, carry):
            part[j, above, c] = (part[j, above, c].astype(f32) + r1[j].astype(f32)).astype(bf16)
            return carry

        lax.fori_loop(0, 4, add_lo, 0)
        zc[1].wait_recv()

        def add_hi(j, carry):
            part[j, below, c] = (part[j, below, c].astype(f32) + r1[j].astype(f32)).astype(bf16)
            return carry

        lax.fori_loop(4, 8, add_hi, 0)

    def factor_gradient(d, recv):
        def tile(i, carry):
            cols = pl.ds(pl.multiple_of(i * 256, 256), 256)
            v = dot(d[...], recv[:, :, cols].reshape(768, 256), TN)
            grad[:, cols] = adapter_scale * v
            return carry

        lax.fori_loop(0, 4, tile, 0)

    with jax.named_scope("forward_above"):
        ag2[3].wait_recv()
        forward(above * 2, False)
        forward(above * 2 + 1, False)

    with jax.named_scope("first_gradient"):
        factor_gradient(dg, recvx)
    da_out = pltpu.make_async_copy(grad, da_hbm, osem.at[0])
    da_out.start()

    with jax.named_scope("rank_sum_x"):
        landed(vrx.at[pl.ds(0, 7)], rk_r.at[2])
        landed(vsx.at[pl.ds(0, 7)], rk_s)
        rank_sum(vsx, vrx, finx)
    x2 = rank_gather(finx, rk_s, rk_r.at[3])
    for copy in x2 + zc[4:]:
        copy.start()

    with jax.named_scope("forward_far"):
        ag2[4].wait_recv()
        ag2[5].wait_recv()
        forward(far * 2, False)
        forward(far * 2 + 1, False)


    with jax.named_scope("wait_rank_x"):
        landed(finx.at[pl.ds(0, 7)], rk_r.at[3])
    with jax.named_scope("lora_out"):
        landed(sendx.at[pl.ds(0, 15)], x_s)
        spread(finx, dx)
        lora(dx, bv, sendx)
    ro = exchange(sendx, reto, ro_s, ro_r)
    for copy in ro:
        copy.start()
    reto[s] = sendx[s]

    with jax.named_scope("second_gradient"):
        da_out.wait()
        factor_gradient(dx, recvg)
    db_out = pltpu.make_async_copy(grad, db_hbm, osem.at[1])
    db_out.start()


    with jax.named_scope("wait_rb"):
        landed(retb.at[pl.ds(0, 15)], rb_r)

    with jax.named_scope("pick_back"):

        def pick(i, carry):
            cols = pl.ds(pl.multiple_of(i * 256, 256), 256)
            v = dot(pt[...], retb[:, :, cols].reshape(768, 256))
            lbs[:, :, cols] = v.astype(bf16).reshape(8, 48, 256)
            return carry

        lax.fori_loop(0, 4, pick, 0)
    lb = [
        remote(lbs.at[(m + k) % 8], lbr.at[m], lb_s, lb_r, mp_dev(k))
        for k in range(1, 8)
    ]
    for copy in lb:
        copy.start()
    lbr[m] = lbs[m]

    with jax.named_scope("wait_ring"):
        landed(part.at[pl.ds(0, 2)], z_r.at[2])
    with jax.named_scope("wait_lb"):
        landed(lbr.at[pl.ds(0, 7)], lb_r)

    with jax.named_scope("input_gradient"):
        for j in range(8):
            v = part[j, z, c].astype(f32) + r2m[j].astype(f32) + r2p[j].astype(f32)
            igb[:, j * 1024 : (j + 1) * 1024] = (v + lbr[j].astype(f32)).astype(bf16)
    ig_out = pltpu.make_async_copy(igb, ig_hbm, osem.at[2])
    ig_out.start()

    with jax.named_scope("wait_ro"):
        landed(reto.at[pl.ds(0, 15)], ro_r)
    with jax.named_scope("output"):

        def finish(i, carry):
            cols = pl.ds(pl.multiple_of(i * 256, 256), 256)
            v = dot(pt[...], reto[:, :, cols].reshape(768, 256))
            outb[:, cols] = (acc[:, cols] + v).astype(bf16)
            pltpu.make_async_copy(outb.at[:, cols], out_hbm.at[:, cols], osem.at[3]).start()
            return carry

        lax.fori_loop(0, 4, finish, 0)

    with jax.named_scope("drain"):
        landed(xall.at[pl.ds(0, 7)], ag_s)
        landed(retb.at[pl.ds(0, 15)], rb_s)
        landed(reto.at[pl.ds(0, 15)], ro_s)
        landed(part.at[pl.ds(0, 3)], z_s)
        landed(vsg.at[pl.ds(0, 7)], rk_s)
        landed(lbs.at[pl.ds(0, 7)], lb_s)
        landed(pr, p_s)
        db_out.wait()
        ig_out.wait()
        landed(outb, osem.at[3])


def hand_over(out, ig, da, db, out_to, ig_to, da_to, db_to, out_v, ig_v, da_v, db_v, sem):
    pieces = []
    for src, via, dst, n in (
        (da, da_v, da_to, 4), (db, db_v, db_to, 4), (out, out_v, out_to, 2), (ig, ig_v, ig_to, 1),
    ):
        rows = src.shape[0] // n
        for h in range(n):
            at = pl.ds(h * rows, rows)
            k = len(pieces)
            pieces.append(
                (
                    pltpu.make_async_copy(src.at[at], via.at[at], sem.at[0, k]),
                    pltpu.make_async_copy(via.at[at], dst.at[at], sem.at[1, k]),
                )
            )
    for come, _ in pieces:
        come.start()
    for come, go in pieces:
        come.wait()
        go.start()
    for _, go in pieces:
        go.wait()


def local(tokens, cotangent, index, storage_row, weight, first_factors, second_factors):
    tok_rows, cols = tokens.shape
    residents, rank, _ = first_factors.shape
    adapters = storage_row.shape[0]
    slots = adapters * max(2, 2 * tok_rows // adapters)
    per = slots // 16
    own = tok_rows // 8
    wide = residents * rank
    anywhere = pl.BlockSpec(memory_space=pl.ANY)
    dma = pltpu.SemaphoreType.DMA
    rows = pltpu.VMEM((16, per, cols), bf16)
    blocks = pltpu.VMEM((8, own, cols), bf16)
    ranks = pltpu.VMEM((8, own, 128), bf16)
    results = pl.pallas_call(
        kernel,
        out_shape=(
            jax.ShapeDtypeStruct((tok_rows, cols), bf16),
            jax.ShapeDtypeStruct((own, 8 * cols), bf16),
            jax.ShapeDtypeStruct((wide, cols), f32),
            jax.ShapeDtypeStruct((wide, cols), f32),
        ),
        in_specs=[anywhere] * 7,
        out_specs=[anywhere] * 4,
        scratch_shapes=[
            pltpu.VMEM((1, tok_rows), i32),
            pltpu.VMEM((1, adapters), i32),
            pltpu.VMEM((8, cols, cols), bf16),
            pltpu.VMEM((8, tok_rows, cols), bf16),
            pltpu.VMEM((tok_rows, cols), bf16),
            pltpu.VMEM((wide, cols), bf16),
            pltpu.VMEM((wide, cols), bf16),
            pltpu.VMEM((tok_rows, slots), bf16),
            pltpu.VMEM((slots, tok_rows), bf16),
            rows, rows, rows, rows, rows, rows,
            pltpu.VMEM((8, 4, 2, own, cols), bf16),
            pltpu.VMEM((8, 4, own, cols), bf16),
            blocks, blocks, blocks, blocks, blocks,
            ranks, ranks, ranks, ranks, ranks, ranks,
            pltpu.VMEM((slots, wide), bf16),
            pltpu.VMEM((slots, wide), bf16),
            pltpu.VMEM((tok_rows, cols), f32),
            pltpu.VMEM((wide, cols), f32),
            pltpu.VMEM((tok_rows, cols), bf16),
            pltpu.VMEM((own, 8 * cols), bf16),
            dma((8,)), dma((6,)), dma((4,)),
            dma, dma((9,)),
            dma, dma, dma, dma, dma, dma, dma, dma,
            dma, dma, dma, dma((3,)),
            dma, dma((4,)),
            dma, dma,
        ],
        compiler_params=pltpu.CompilerParams(
            collective_id=0, has_side_effects=True, vmem_limit_bytes=62 * 2**20
        ),
        cost_estimate=pl.CostEstimate(
            flops=20_000_000_000, bytes_accessed=30_000_000, transcendentals=0
        ),
        name="adapter_step",
    )(
        index.reshape(1, tok_rows),
        storage_row.reshape(1, adapters),
        tokens,
        cotangent,
        weight.reshape(8, cols, cols),
        first_factors.reshape(wide, cols),
        second_factors.reshape(wide, cols),
    )
    output, input_gradient, first_gradient, second_gradient = pl.pallas_call(
        hand_over,
        out_shape=tuple(jax.ShapeDtypeStruct(r.shape, r.dtype) for r in results),
        in_specs=[anywhere] * 4,
        out_specs=[anywhere] * 4,
        scratch_shapes=[pltpu.VMEM(r.shape, r.dtype) for r in results] + [dma((2, 11))],
        compiler_params=pltpu.CompilerParams(vmem_limit_bytes=62 * 2**20),
        name="hand_over",
    )(*results)
    shape = first_factors.shape
    return output, input_gradient, first_gradient.reshape(shape), second_gradient.reshape(shape)


def solution(mesh):
    in_specs = (
        P("dp", "mp"),
        P("dp", "mp"),
        P("dp", None),
        P(),
        P(None, "mp"),
        P("dp", None, "mp"),
        P("dp", None, "mp"),
    )
    out_specs = (P("dp", "mp"), P(("dp", "mp"), None), P("dp", None, "mp"), P("dp", None, "mp"))
    return jax.shard_map(local, mesh=mesh, in_specs=in_specs, out_specs=out_specs, check_vma=False)
```

time: 116 us -> 96.1 us (0.83)
  Pallas kernels: 105 us -> 95.4 us
  local copies, waits for them, and re-layouts: 9.44 us -> 0 us
    pallas_call x1, Pallas kernels: 105 us -> 90 us  [local(): pl.pallas_call(kernel, out_shape=(jax.ShapeDtypeStruct((tok_rows, cols),...]
    unnamed x9 -> x0, local copies, waits for them, and re-layouts: 9.44 us -> none
    pallas_call x0 -> x1, Pallas kernels: none -> 5.35 us  [local(): pl.pallas_call(hand_over, out_shape=tuple((jax.ShapeDtypeStruct(r.shape,...]
where the time goes in v2:
time: 96.1 us; the launch traced here: 96 us
  Pallas kernels  95.4 us (99%)
    pallas_call x1, Pallas kernels, local(): pl.pallas_call(kernel, out_shape=(jax.ShapeDtypeStruct((tok_rows, cols),...  90 us
    pallas_call x1, Pallas kernels, local(): pl.pallas_call(hand_over, out_shape=tuple((jax.ShapeDtypeStruct(r.shape,...  5.35 us

profile of v2, /device:TPU:1, one launch (start us, length us, event | category | flops | bytes accessed | tf_op | source)
XLA Modules:
  0.0 96.0 jit_solution(13449017425574909988)
XLA Ops:
  0.6 90.0 %adapter_step.1 = (bf16[384,1024]{1,0:T(8,128)(2,1)}, bf16[48,8192]{1,0:T(8,128)(2,1)}, f32[512,1024]{1,0:T(8,128)}, f32[512,1024]{1,0:T(8,128)}) custom-call(s32[1,384]{1,0:T(1,128)} %bitcast.12, s32[1,128]{1,0:T(1,128)} %bitcast.13, bf16[384,1024]{1,0:T(8,128)(2,1)} %tok_hbm.1, bf16[384,1024]{1,0:T(8,128)(2,1)} %cot_hbm.1, bf16[8,1024,1024]{2,1,0:T(8,128)(2,1)} %bitcast.7, ...), custom_call_target="tpu_custom_call" | custom-call | flops 20000000000 | bytes 30000000 | tf_op jit(solution)/shard_map/adapter_step/pallas_call | solution.py:477
  90.6 5.4 %hand_over.1 = (bf16[384,1024]{1,0:T(8,128)(2,1)}, bf16[48,8192]{1,0:T(8,128)(2,1)}, f32[512,1024]{1,0:T(8,128)}, f32[512,1024]{1,0:T(8,128)}) custom-call(bf16[384,1024]{1,0:T(8,128)(2,1)} %get-tuple-element.12.out, bf16[48,8192]{1,0:T(8,128)(2,1)} %get-tuple-element.13.ig, f32[512,1024]{1,0:T(8,128)} %get-tuple-element.14.da, f32[512,1024]{1,0:T(8,128)} %get-tuple-element.15.db), custom_call_target="tpu_custom_call" | custom-call | tf_op jit(solution)/shard_map/hand_over/pallas_call | solution.py:531

commit v3 on v2

--- a/solution.py
+++ b/solution.py
@@ -23,11 +23,10 @@
 
 def kernel(
     idx_hbm, row_hbm, tok_hbm, cot_hbm, w_hbm, a_hbm, b_hbm,
-    out_hbm, ig_hbm, da_hbm, db_hbm,
+    outb, igb, da, db,
     idx_ref, row_ref, wv, xall, cot, av, bv, pt, pm, sendg, sendx, recvg, recvx, retb, reto,
     part, pr, r1, r2m, r2p, lbs, lbr, vsg, vrg, fing, vsx, vrx, finx, dg, dx, acc,
-    grad, outb, igb,
-    wsem, lsem, osem, ag_s, ag_r, g_s, g_r, x_s, x_r, rb_s, rb_r, ro_s, ro_r,
+    wsem, lsem, ag_s, ag_r, g_s, g_r, x_s, x_r, rb_s, rb_r, ro_s, ro_r,
     p_s, p_r, z_s, z_r, rk_s, rk_r, lb_s, lb_r,
 ):
     s, m = lax.axis_index("dp"), lax.axis_index("mp")
@@ -171,6 +170,19 @@
     with jax.named_scope("pair_sum"):
         landed(pr, p_r)
         lax.fori_loop(0, 8, pair_sum, 0)
+    below, above, far = (z + 3) % 4, (z + 1) % 4, (z + 2) % 4
+    lo, hi = pl.ds(0, 4), pl.ds(4, 4)
+    zc = [
+        remote(part.at[lo, far, c], r1.at[lo], z_s, z_r.at[0], zdev(1)),
+        remote(part.at[hi, far, c], r1.at[hi], z_s, z_r.at[1], zdev(3)),
+        remote(part.at[hi, above, c], r2m.at[hi], z_s, z_r.at[2], zdev(1)),
+        remote(part.at[lo, below, c], r2p.at[lo], z_s, z_r.at[2], zdev(3)),
+        remote(part.at[lo, above, c], r2m.at[lo], z_s, z_r.at[2], zdev(1)),
+        remote(part.at[hi, below, c], r2p.at[hi], z_s, z_r.at[2], zdev(3)),
+    ]
+    for copy in zc[:2]:
+        copy.start()
+
     def forward(slot, start):
         def tile(i, carry):
             cols = pl.ds(pl.multiple_of(i * 256, 256), 256)
@@ -185,7 +197,6 @@
         ag[2].wait_recv()
         forward(m + 1 - 2 * c, False)
 
-    below, above, far = (z + 3) % 4, (z + 1) % 4, (z + 2) % 4
     lo_rows, hi_rows = pl.ds(0, tok_rows // 2), pl.ds(tok_rows // 2, tok_rows // 2)
     row48 = lax.broadcasted_iota(i32, (48, 512), 0)
     first = (lax.broadcasted_iota(i32, (48, 512), 1) >> 6) * capacity
@@ -234,15 +245,14 @@
     for copy in g1:
         copy.start()
 
-    lo, hi = pl.ds(0, 4), pl.ds(4, 4)
-    zc = [
-        remote(part.at[lo, far, c], r1.at[lo], z_s, z_r.at[0], zdev(1)),
-        remote(part.at[hi, far, c], r1.at[hi], z_s, z_r.at[1], zdev(3)),
-        remote(part.at[hi, above, c], r2m.at[hi], z_s, z_r.at[2], zdev(1)),
-        remote(part.at[lo, below, c], r2p.at[lo], z_s, z_r.at[2], zdev(3)),
-        remote(part.at[lo, above, c], r2m.at[lo], z_s, z_r.at[2], zdev(1)),
-        remote(part.at[hi, below, c], r2p.at[hi], z_s, z_r.at[2], zdev(3)),
-    ]
+    with jax.named_scope("rank_sum_g"):
+        landed(vrg.at[pl.ds(0, 7)], rk_r.at[0])
+        landed(vsg.at[pl.ds(0, 7)], rk_s)
+        rank_sum(vsg, vrg, fing)
+    g2 = rank_gather(fing, rk_s, rk_r.at[1])
+    for copy in g2:
+        copy.start()
+
     with jax.named_scope("tokens_forward"):
         ag[0].wait_recv()
         from_below, from_above = xall.at[below * 2 + c], xall.at[above * 2 + c]
@@ -261,13 +271,6 @@
         ag2[1].start()
         ag2[3].start()
 
-    with jax.named_scope("rank_sum_g"):
-        landed(vrg.at[pl.ds(0, 7)], rk_r.at[0])
-        landed(vsg.at[pl.ds(0, 7)], rk_s)
-        rank_sum(vsg, vrg, fing)
-    g2 = rank_gather(fing, rk_s, rk_r.at[1])
-    for copy in g2 + zc[:2]:
-        copy.start()
 
     a_in.wait()
     with jax.named_scope("wait_rank_g"):
@@ -297,7 +300,45 @@
     with jax.named_scope("project_x"):
         project(recvx, av, vsx)
     x1 = rank_scatter(vsx, vrx, rk_s, rk_r.at[2])
-    for copy in x1 + zc[2:4]:
+    for copy in x1:
+        copy.start()
+
+    def factor_gradient(d, recv, grad):
+        def tile(i, carry):
+            cols = pl.ds(pl.multiple_of(i * 256, 256), 256)
+            v = dot(d[...], recv[:, :, cols].reshape(768, 256), TN)
+            grad[:, cols] = adapter_scale * v
+            return carry
+
+        lax.fori_loop(0, 4, tile, 0)
+
+    with jax.named_scope("ring_second"):
+        zc[0].wait_recv()
+
+        def add_lo(j, carry):
+            part[j, above, c] = (part[j, above, c].astype(f32) + r1[j].astype(f32)).astype(bf16)
+            return carry
+
+        lax.fori_loop(0, 4, add_lo, 0)
+        zc[1].wait_recv()
+
+        def add_hi(j, carry):
+            part[j, below, c] = (part[j, below, c].astype(f32) + r1[j].astype(f32)).astype(bf16)
+            return carry
+
+        lax.fori_loop(4, 8, add_hi, 0)
+
+    with jax.named_scope("forward_below"):
+        ag2[2].wait_recv()
+        forward(below * 2, False)
+        forward(below * 2 + 1, False)
+
+    with jax.named_scope("rank_sum_x"):
+        landed(vrx.at[pl.ds(0, 7)], rk_r.at[2])
+        landed(vsx.at[pl.ds(0, 7)], rk_s)
+        rank_sum(vsx, vrx, finx)
+    x2 = rank_gather(finx, rk_s, rk_r.at[3])
+    for copy in x2 + zc[2:]:
         copy.start()
 
     with jax.named_scope("tokens_far"):
@@ -306,60 +347,10 @@
         ag2[1].wait_recv()
         ag2[5].start()
 
-    with jax.named_scope("forward_below"):
-        ag2[2].wait_recv()
-        forward(below * 2, False)
-        forward(below * 2 + 1, False)
-
-    with jax.named_scope("ring_second"):
-        zc[0].wait_recv()
-
-        def add_lo(j, carry):
-            part[j, above, c] = (part[j, above, c].astype(f32) + r1[j].astype(f32)).astype(bf16)
-            return carry
-
-        lax.fori_loop(0, 4, add_lo, 0)
-        zc[1].wait_recv()
-
-        def add_hi(j, carry):
-            part[j, below, c] = (part[j, below, c].astype(f32) + r1[j].astype(f32)).astype(bf16)
-            return carry
-
-        lax.fori_loop(4, 8, add_hi, 0)
-
-    def factor_gradient(d, recv):
-        def tile(i, carry):
-            cols = pl.ds(pl.multiple_of(i * 256, 256), 256)
-            v = dot(d[...], recv[:, :, cols].reshape(768, 256), TN)
-            grad[:, cols] = adapter_scale * v
-            return carry
-
-        lax.fori_loop(0, 4, tile, 0)
-
     with jax.named_scope("forward_above"):
         ag2[3].wait_recv()
         forward(above * 2, False)
         forward(above * 2 + 1, False)
-
-    with jax.named_scope("first_gradient"):
-        factor_gradient(dg, recvx)
-    da_out = pltpu.make_async_copy(grad, da_hbm, osem.at[0])
-    da_out.start()
-
-    with jax.named_scope("rank_sum_x"):
-        landed(vrx.at[pl.ds(0, 7)], rk_r.at[2])
-        landed(vsx.at[pl.ds(0, 7)], rk_s)
-        rank_sum(vsx, vrx, finx)
-    x2 = rank_gather(finx, rk_s, rk_r.at[3])
-    for copy in x2 + zc[4:]:
-        copy.start()
-
-    with jax.named_scope("forward_far"):
-        ag2[4].wait_recv()
-        ag2[5].wait_recv()
-        forward(far * 2, False)
-        forward(far * 2 + 1, False)
-
 
     with jax.named_scope("wait_rank_x"):
         landed(finx.at[pl.ds(0, 7)], rk_r.at[3])
@@ -372,11 +363,18 @@
         copy.start()
     reto[s] = sendx[s]
 
+    with jax.named_scope("first_gradient"):
+        factor_gradient(dg, recvx, da)
+
     with jax.named_scope("second_gradient"):
-        da_out.wait()
-        factor_gradient(dx, recvg)
-    db_out = pltpu.make_async_copy(grad, db_hbm, osem.at[1])
-    db_out.start()
+        factor_gradient(dx, recvg, db)
+
+
+    with jax.named_scope("forward_far"):
+        ag2[4].wait_recv()
+        ag2[5].wait_recv()
+        forward(far * 2, False)
+        forward(far * 2 + 1, False)
 
 
     with jax.named_scope("wait_rb"):
@@ -408,8 +406,6 @@
         for j in range(8):
             v = part[j, z, c].astype(f32) + r2m[j].astype(f32) + r2p[j].astype(f32)
             igb[:, j * 1024 : (j + 1) * 1024] = (v + lbr[j].astype(f32)).astype(bf16)
-    ig_out = pltpu.make_async_copy(igb, ig_hbm, osem.at[2])
-    ig_out.start()
 
     with jax.named_scope("wait_ro"):
         landed(reto.at[pl.ds(0, 15)], ro_r)
@@ -419,7 +415,6 @@
             cols = pl.ds(pl.multiple_of(i * 256, 256), 256)
             v = dot(pt[...], reto[:, :, cols].reshape(768, 256))
             outb[:, cols] = (acc[:, cols] + v).astype(bf16)
-            pltpu.make_async_copy(outb.at[:, cols], out_hbm.at[:, cols], osem.at[3]).start()
             return carry
 
         lax.fori_loop(0, 4, finish, 0)
@@ -432,33 +427,19 @@
         landed(vsg.at[pl.ds(0, 7)], rk_s)
         landed(lbs.at[pl.ds(0, 7)], lb_s)
         landed(pr, p_s)
-        db_out.wait()
-        ig_out.wait()
-        landed(outb, osem.at[3])
-
-
-def hand_over(out, ig, da, db, out_to, ig_to, da_to, db_to, out_v, ig_v, da_v, db_v, sem):
-    pieces = []
-    for src, via, dst, n in (
-        (da, da_v, da_to, 4), (db, db_v, db_to, 4), (out, out_v, out_to, 2), (ig, ig_v, ig_to, 1),
-    ):
+
+
+def hand_over(out, ig, da, db, out_to, ig_to, da_to, db_to, sem):
+    copies = []
+    for src, dst, n in ((da, da_to, 4), (db, db_to, 4), (out, out_to, 2), (ig, ig_to, 1)):
         rows = src.shape[0] // n
         for h in range(n):
             at = pl.ds(h * rows, rows)
-            k = len(pieces)
-            pieces.append(
-                (
-                    pltpu.make_async_copy(src.at[at], via.at[at], sem.at[0, k]),
-                    pltpu.make_async_copy(via.at[at], dst.at[at], sem.at[1, k]),
-                )
-            )
-    for come, _ in pieces:
-        come.start()
-    for come, go in pieces:
-        come.wait()
-        go.start()
-    for _, go in pieces:
-        go.wait()
+            copies.append(pltpu.make_async_copy(src.at[at], dst.at[at], sem.at[len(copies)]))
+    for copy in copies:
+        copy.start()
+    for copy in copies:
+        copy.wait()
 
 
 def local(tokens, cotangent, index, storage_row, weight, first_factors, second_factors):
@@ -477,13 +458,13 @@
     results = pl.pallas_call(
         kernel,
         out_shape=(
-            jax.ShapeDtypeStruct((tok_rows, cols), bf16),
-            jax.ShapeDtypeStruct((own, 8 * cols), bf16),
-            jax.ShapeDtypeStruct((wide, cols), f32),
-            jax.ShapeDtypeStruct((wide, cols), f32),
+            pltpu.VMEM((tok_rows, cols), bf16),
+            pltpu.VMEM((own, 8 * cols), bf16),
+            pltpu.VMEM((wide, cols), f32),
+            pltpu.VMEM((wide, cols), f32),
         ),
         in_specs=[anywhere] * 7,
-        out_specs=[anywhere] * 4,
+        out_specs=[pl.BlockSpec(memory_space=pltpu.VMEM)] * 4,
         scratch_shapes=[
             pltpu.VMEM((1, tok_rows), i32),
             pltpu.VMEM((1, adapters), i32),
@@ -502,10 +483,7 @@
             pltpu.VMEM((slots, wide), bf16),
             pltpu.VMEM((slots, wide), bf16),
             pltpu.VMEM((tok_rows, cols), f32),
-            pltpu.VMEM((wide, cols), f32),
-            pltpu.VMEM((tok_rows, cols), bf16),
-            pltpu.VMEM((own, 8 * cols), bf16),
-            dma((8,)), dma((6,)), dma((4,)),
+            dma((8,)), dma((6,)),
             dma, dma((9,)),
             dma, dma, dma, dma, dma, dma, dma, dma,
             dma, dma, dma, dma((3,)),
@@ -513,7 +491,7 @@
             dma, dma,
         ],
         compiler_params=pltpu.CompilerParams(
-            collective_id=0, has_side_effects=True, vmem_limit_bytes=62 * 2**20
+            collective_id=0, has_side_effects=True, vmem_limit_bytes=56 * 2**20
         ),
         cost_estimate=pl.CostEstimate(
             flops=20_000_000_000, bytes_accessed=30_000_000, transcendentals=0
@@ -531,10 +509,10 @@
     output, input_gradient, first_gradient, second_gradient = pl.pallas_call(
         hand_over,
         out_shape=tuple(jax.ShapeDtypeStruct(r.shape, r.dtype) for r in results),
-        in_specs=[anywhere] * 4,
+        in_specs=[pl.BlockSpec(memory_space=pltpu.VMEM)] * 4,
         out_specs=[anywhere] * 4,
-        scratch_shapes=[pltpu.VMEM(r.shape, r.dtype) for r in results] + [dma((2, 11))],
-        compiler_params=pltpu.CompilerParams(vmem_limit_bytes=62 * 2**20),
+        scratch_shapes=[dma((11,))],
+        compiler_params=pltpu.CompilerParams(vmem_limit_bytes=16 * 2**20),
         name="hand_over",
     )(*results)
     shape = first_factors.shape

time: 96.1 us -> 88.9 us (0.925)
  Pallas kernels: 95.4 us -> 87.4 us
    pallas_call x1, Pallas kernels: 90 us -> 84.9 us  [local(): pl.pallas_call(kernel, out_shape=(pltpu.VMEM((tok_rows, cols), bf16), plt...]
    pallas_call x1, Pallas kernels: 5.35 us -> 2.59 us  [local(): pl.pallas_call(hand_over, out_shape=tuple((jax.ShapeDtypeStruct(r.shape,...]
where the time goes in v3:
time: 88.9 us; the launch traced here: 88.1 us
  Pallas kernels  87.4 us (98%)
    pallas_call x1, Pallas kernels, local(): pl.pallas_call(kernel, out_shape=(pltpu.VMEM((tok_rows, cols), bf16), plt...  84.9 us
    pallas_call x1, Pallas kernels, local(): pl.pallas_call(hand_over, out_shape=tuple((jax.ShapeDtypeStruct(r.shape,...  2.59 us

profile of v3, /device:TPU:1, one launch (start us, length us, event | category | flops | bytes accessed | tf_op | source)
XLA Modules:
  0.0 88.1 jit_solution(12209966635463807966)
XLA Ops:
  0.6 84.9 %adapter_step.1 = (bf16[384,1024]{1,0:T(8,128)(2,1)S(1)}, bf16[48,8192]{1,0:T(8,128)(2,1)S(1)}, f32[512,1024]{1,0:T(8,128)S(1)}, f32[512,1024]{1,0:T(8,128)S(1)}) custom-call(s32[1,384]{1,0:T(1,128)} %bitcast.12, s32[1,128]{1,0:T(1,128)} %bitcast.13, bf16[384,1024]{1,0:T(8,128)(2,1)} %tok_hbm.1, bf16[384,1024]{1,0:T(8,128)(2,1)} %cot_hbm.1, ...), custom_call_target="tpu_custom_call" | custom-call | flops 20000000000 | bytes 30000000 | tf_op jit(solution)/shard_map/adapter_step/pallas_call | solution.py:458
  85.5 2.6 %hand_over.1 = (bf16[384,1024]{1,0:T(8,128)(2,1)}, bf16[48,8192]{1,0:T(8,128)(2,1)}, f32[512,1024]{1,0:T(8,128)}, f32[512,1024]{1,0:T(8,128)}) custom-call(bf16[384,1024]{1,0:T(8,128)(2,1)S(1)} %get-tuple-element.12.out, bf16[48,8192]{1,0:T(8,128)(2,1)S(1)} %get-tuple-element.13.ig, f32[512,1024]{1,0:T(8,128)S(1)} %get-tuple-element.14.da, ...), custom_call_target="tpu_custom_call" | custom-call | tf_op jit(solution)/shard_map/hand_over/pallas_call | solution.py:509

commit v4 on v3

--- a/solution.py
+++ b/solution.py
@@ -10,8 +10,8 @@
 bf16, f32, i32 = jnp.bfloat16, jnp.float32, jnp.int32
 
 OFFSETS = (
-    (1, 0), (3, 0), (0, 1), (0, 3), (2, 2), (1, 1), (3, 3), (1, 3),
-    (3, 1), (2, 0), (0, 2), (2, 1), (1, 2), (2, 3), (3, 2),
+    (1, 0), (3, 0), (0, 1), (0, 3), (2, 2), (1, 1), (3, 3), (2, 0),
+    (0, 2), (1, 3), (3, 1), (2, 1), (1, 2), (2, 3), (3, 2),
 )
 NT = (((1,), (1,)), ((), ()))
 TN = (((0,), (0,)), ((), ()))
@@ -23,9 +23,9 @@
 
 def kernel(
     idx_hbm, row_hbm, tok_hbm, cot_hbm, w_hbm, a_hbm, b_hbm,
-    outb, igb, da, db,
-    idx_ref, row_ref, wv, xall, cot, av, bv, pt, pm, sendg, sendx, recvg, recvx, retb, reto,
-    part, pr, r1, r2m, r2p, lbs, lbr, vsg, vrg, fing, vsx, vrx, finx, dg, dx, acc,
+    igb, da, db, acc, reto, pt,
+    idx_ref, row_ref, wv, xall, cot, av, bv, pm, sendg, sendx, recvg, recvx, retb,
+    part, pr, r1, r2m, r2p, lbs, lbx, r3, vsg, vrg, fing, vsx, vrx, finx, dg, dx,
     wsem, lsem, ag_s, ag_r, g_s, g_r, x_s, x_r, rb_s, rb_r, ro_s, ro_r,
     p_s, p_r, z_s, z_r, rk_s, rk_r, lb_s, lb_r,
 ):
@@ -51,7 +51,11 @@
 
     def exchange(send, recv, ss, rs):
         return [
-            remote(send.at[dp_at(k)], recv.at[s], ss, rs, {"dp": dp_at(k), "mp": m})
+            remote(
+                send.at[dp_at(k), pl.ds(16 * r, 16)], recv.at[s, pl.ds(16 * r, 16)], ss, rs,
+                {"dp": dp_at(k), "mp": m},
+            )
+            for r in range(3)
             for k in range(15)
         ]
 
@@ -154,13 +158,13 @@
         return carry
 
     with jax.named_scope("frozen_back"):
-        lax.fori_loop(0, 5, frozen_back, 0)
+        lax.fori_loop(0, 7, frozen_back, 0)
 
     x_x = exchange(sendx, recvx, x_s, x_r)
     for copy in x_x:
         copy.start()
     with jax.named_scope("frozen_back_2"):
-        lax.fori_loop(5, 8, frozen_back, 0)
+        lax.fori_loop(7, 8, frozen_back, 0)
 
     def pair_sum(j, carry):
         for q in range(4):
@@ -171,17 +175,20 @@
         landed(pr, p_r)
         lax.fori_loop(0, 8, pair_sum, 0)
     below, above, far = (z + 3) % 4, (z + 1) % 4, (z + 2) % 4
-    lo, hi = pl.ds(0, 4), pl.ds(4, 4)
-    zc = [
-        remote(part.at[lo, far, c], r1.at[lo], z_s, z_r.at[0], zdev(1)),
-        remote(part.at[hi, far, c], r1.at[hi], z_s, z_r.at[1], zdev(3)),
-        remote(part.at[hi, above, c], r2m.at[hi], z_s, z_r.at[2], zdev(1)),
-        remote(part.at[lo, below, c], r2p.at[lo], z_s, z_r.at[2], zdev(3)),
-        remote(part.at[lo, above, c], r2m.at[lo], z_s, z_r.at[2], zdev(1)),
-        remote(part.at[hi, below, c], r2p.at[hi], z_s, z_r.at[2], zdev(3)),
-    ]
-    for copy in zc[:2]:
-        copy.start()
+    zfirst = []
+    for h in range(2):
+        lo, hi = pl.ds(2 * h, 2), pl.ds(4 + 2 * h, 2)
+        zfirst.append(remote(part.at[lo, far, c], r1.at[lo], z_s, z_r.at[0], zdev(1)))
+        zfirst.append(remote(part.at[hi, far, c], r1.at[hi], z_s, z_r.at[1], zdev(3)))
+    zfirst[0].start()
+    zfirst[1].start()
+
+    def zsecond(step):
+        pair_of = pl.ds((z + step) % 4 * 2, 2)
+        return [
+            remote(part.at[pair_of, above, c], r2m.at[pair_of], z_s, z_r.at[2], zdev(1)),
+            remote(part.at[pair_of, below, c], r2p.at[pair_of], z_s, z_r.at[2], zdev(3)),
+        ]
 
     def forward(slot, start):
         def tile(i, carry):
@@ -250,7 +257,7 @@
         landed(vsg.at[pl.ds(0, 7)], rk_s)
         rank_sum(vsg, vrg, fing)
     g2 = rank_gather(fing, rk_s, rk_r.at[1])
-    for copy in g2:
+    for copy in g2 + zfirst[2:]:
         copy.start()
 
     with jax.named_scope("tokens_forward"):
@@ -313,14 +320,14 @@
         lax.fori_loop(0, 4, tile, 0)
 
     with jax.named_scope("ring_second"):
-        zc[0].wait_recv()
+        landed(r1.at[pl.ds(0, 4)], z_r.at[0])
 
         def add_lo(j, carry):
             part[j, above, c] = (part[j, above, c].astype(f32) + r1[j].astype(f32)).astype(bf16)
             return carry
 
         lax.fori_loop(0, 4, add_lo, 0)
-        zc[1].wait_recv()
+        landed(r1.at[pl.ds(4, 4)], z_r.at[1])
 
         def add_hi(j, carry):
             part[j, below, c] = (part[j, below, c].astype(f32) + r1[j].astype(f32)).astype(bf16)
@@ -338,7 +345,7 @@
         landed(vsx.at[pl.ds(0, 7)], rk_s)
         rank_sum(vsx, vrx, finx)
     x2 = rank_gather(finx, rk_s, rk_r.at[3])
-    for copy in x2 + zc[2:]:
+    for copy in x2 + zsecond(1) + zsecond(2) + zsecond(3):
         copy.start()
 
     with jax.named_scope("tokens_far"):
@@ -385,59 +392,67 @@
         def pick(i, carry):
             cols = pl.ds(pl.multiple_of(i * 256, 256), 256)
             v = dot(pt[...], retb[:, :, cols].reshape(768, 256))
-            lbs[:, :, cols] = v.astype(bf16).reshape(8, 48, 256)
+            lbs[:, :, :, cols] = v.astype(bf16).reshape(4, 2, 48, 256)
             return carry
 
         lax.fori_loop(0, 4, pick, 0)
-    lb = [
-        remote(lbs.at[(m + k) % 8], lbr.at[m], lb_s, lb_r, mp_dev(k))
-        for k in range(1, 8)
+    across = remote(lbs.at[:, 1 - c], lbx, lb_s, lb_r.at[0], zdev(0, 1))
+    across.start()
+    own, other = m, m + 1 - 2 * c
+    with jax.named_scope("add_back"):
+        for q in (z, above, below):
+            part[own, q, c] = (part[own, q, c].astype(f32) + lbs[q, c].astype(f32)).astype(bf16)
+        landed(lbx, lb_r.at[0])
+        for q in (z, above, below):
+            part[other, q, c] = (part[other, q, c].astype(f32) + lbx[q].astype(f32)).astype(bf16)
+    late = zsecond(0) + [
+        remote(lbs.at[far, c], r3.at[c], lb_s, lb_r.at[1], zdev(2)),
+        remote(lbx.at[far], r3.at[1 - c], lb_s, lb_r.at[1], zdev(2)),
     ]
-    for copy in lb:
-        copy.start()
-    lbr[m] = lbs[m]
+    for copy in late:
+        copy.start()
 
     with jax.named_scope("wait_ring"):
         landed(part.at[pl.ds(0, 2)], z_r.at[2])
-    with jax.named_scope("wait_lb"):
-        landed(lbr.at[pl.ds(0, 7)], lb_r)
+        landed(r3, lb_r.at[1])
 
     with jax.named_scope("input_gradient"):
+        for h in range(2):
+            k = far * 2 + h
+            part[k, z, c] = (part[k, z, c].astype(f32) + r3[h].astype(f32)).astype(bf16)
         for j in range(8):
             v = part[j, z, c].astype(f32) + r2m[j].astype(f32) + r2p[j].astype(f32)
-            igb[:, j * 1024 : (j + 1) * 1024] = (v + lbr[j].astype(f32)).astype(bf16)
+            igb[:, j * 1024 : (j + 1) * 1024] = v.astype(bf16)
 
     with jax.named_scope("wait_ro"):
         landed(reto.at[pl.ds(0, 15)], ro_r)
-    with jax.named_scope("output"):
-
-        def finish(i, carry):
-            cols = pl.ds(pl.multiple_of(i * 256, 256), 256)
-            v = dot(pt[...], reto[:, :, cols].reshape(768, 256))
-            outb[:, cols] = (acc[:, cols] + v).astype(bf16)
-            return carry
-
-        lax.fori_loop(0, 4, finish, 0)
-
     with jax.named_scope("drain"):
         landed(xall.at[pl.ds(0, 7)], ag_s)
         landed(retb.at[pl.ds(0, 15)], rb_s)
         landed(reto.at[pl.ds(0, 15)], ro_s)
         landed(part.at[pl.ds(0, 3)], z_s)
         landed(vsg.at[pl.ds(0, 7)], rk_s)
-        landed(lbs.at[pl.ds(0, 7)], lb_s)
+        landed(lbx, lb_s)
+        landed(r3, lb_s)
         landed(pr, p_s)
 
 
-def hand_over(out, ig, da, db, out_to, ig_to, da_to, db_to, sem):
+def hand_over(ig, da, db, acc, back, pt, out_to, ig_to, da_to, db_to, out, sem):
     copies = []
-    for src, dst, n in ((da, da_to, 4), (db, db_to, 4), (out, out_to, 2), (ig, ig_to, 1)):
+    for src, dst, n in ((ig, ig_to, 1), (da, da_to, 4), (db, db_to, 4)):
         rows = src.shape[0] // n
         for h in range(n):
             at = pl.ds(h * rows, rows)
             copies.append(pltpu.make_async_copy(src.at[at], dst.at[at], sem.at[len(copies)]))
     for copy in copies:
         copy.start()
+    for i in range(4):
+        cols = pl.ds(256 * i, 256)
+        v = dot(pt[...], back[:, :, cols].reshape(pt.shape[1], 256))
+        out[:, cols] = (acc[:, cols] + v).astype(bf16)
+        copy = pltpu.make_async_copy(out.at[:, cols], out_to.at[:, cols], sem.at[len(copies)])
+        copy.start()
+        copies.append(copy)
     for copy in copies:
         copy.wait()
 
@@ -451,6 +466,7 @@
     own = tok_rows // 8
     wide = residents * rank
     anywhere = pl.BlockSpec(memory_space=pl.ANY)
+    vmem = pl.BlockSpec(memory_space=pltpu.VMEM)
     dma = pltpu.SemaphoreType.DMA
     rows = pltpu.VMEM((16, per, cols), bf16)
     blocks = pltpu.VMEM((8, own, cols), bf16)
@@ -458,13 +474,15 @@
     results = pl.pallas_call(
         kernel,
         out_shape=(
-            pltpu.VMEM((tok_rows, cols), bf16),
             pltpu.VMEM((own, 8 * cols), bf16),
             pltpu.VMEM((wide, cols), f32),
             pltpu.VMEM((wide, cols), f32),
+            pltpu.VMEM((tok_rows, cols), f32),
+            rows,
+            pltpu.VMEM((tok_rows, slots), bf16),
         ),
         in_specs=[anywhere] * 7,
-        out_specs=[pl.BlockSpec(memory_space=pltpu.VMEM)] * 4,
+        out_specs=[vmem] * 6,
         scratch_shapes=[
             pltpu.VMEM((1, tok_rows), i32),
             pltpu.VMEM((1, adapters), i32),
@@ -473,25 +491,26 @@
             pltpu.VMEM((tok_rows, cols), bf16),
             pltpu.VMEM((wide, cols), bf16),
             pltpu.VMEM((wide, cols), bf16),
-            pltpu.VMEM((tok_rows, slots), bf16),
             pltpu.VMEM((slots, tok_rows), bf16),
-            rows, rows, rows, rows, rows, rows,
+            rows, rows, rows, rows, rows,
             pltpu.VMEM((8, 4, 2, own, cols), bf16),
             pltpu.VMEM((8, 4, own, cols), bf16),
-            blocks, blocks, blocks, blocks, blocks,
+            blocks, blocks, blocks,
+            pltpu.VMEM((4, 2, own, cols), bf16),
+            pltpu.VMEM((4, own, cols), bf16),
+            pltpu.VMEM((2, own, cols), bf16),
             ranks, ranks, ranks, ranks, ranks, ranks,
             pltpu.VMEM((slots, wide), bf16),
             pltpu.VMEM((slots, wide), bf16),
-            pltpu.VMEM((tok_rows, cols), f32),
             dma((8,)), dma((6,)),
             dma, dma((9,)),
             dma, dma, dma, dma, dma, dma, dma, dma,
             dma, dma, dma, dma((3,)),
             dma, dma((4,)),
-            dma, dma,
+            dma, dma((2,)),
         ],
         compiler_params=pltpu.CompilerParams(
-            collective_id=0, has_side_effects=True, vmem_limit_bytes=56 * 2**20
+            collective_id=0, has_side_effects=True, vmem_limit_bytes=54 * 2**20
         ),
         cost_estimate=pl.CostEstimate(
             flops=20_000_000_000, bytes_accessed=30_000_000, transcendentals=0
@@ -508,10 +527,15 @@
     )
     output, input_gradient, first_gradient, second_gradient = pl.pallas_call(
         hand_over,
-        out_shape=tuple(jax.ShapeDtypeStruct(r.shape, r.dtype) for r in results),
-        in_specs=[pl.BlockSpec(memory_space=pltpu.VMEM)] * 4,
+        out_shape=(
+            jax.ShapeDtypeStruct(tokens.shape, bf16),
+            jax.ShapeDtypeStruct((own, 8 * cols), bf16),
+            jax.ShapeDtypeStruct((wide, cols), f32),
+            jax.ShapeDtypeStruct((wide, cols), f32),
+        ),
+        in_specs=[vmem] * 6,
         out_specs=[anywhere] * 4,
-        scratch_shapes=[dma((11,))],
+        scratch_shapes=[pltpu.VMEM(tokens.shape, bf16), dma((13,))],
         compiler_params=pltpu.CompilerParams(vmem_limit_bytes=16 * 2**20),
         name="hand_over",
     )(*results)

time: 88.9 us -> 83.7 us (0.942)
  Pallas kernels: 87.4 us -> 82.9 us
    pallas_call x2, Pallas kernels: 87.4 us -> 82.9 us  [the longest x1 80.3 us: local(): pl.pallas_call(kernel, out_shape=(pltpu.VMEM((own, 8 * cols), bf16), pltp...]
where the time goes in v4:
time: 83.7 us; the launch traced here: 83.6 us
  Pallas kernels  82.9 us (99%)
    pallas_call x1, Pallas kernels, local(): pl.pallas_call(kernel, out_shape=(pltpu.VMEM((own, 8 * cols), bf16), pltp...  80.3 us
    pallas_call x1, Pallas kernels, local(): pl.pallas_call(hand_over, out_shape=(jax.ShapeDtypeStruct(tokens.shape, b...  2.59 us

profile of v4, /device:TPU:1, one launch (start us, length us, event | category | flops | bytes accessed | tf_op | source)
XLA Modules:
  0.0 83.6 jit_solution(3464042095613902331)
XLA Ops:
  0.6 80.3 %adapter_step.1 = (bf16[48,8192]{1,0:T(8,128)(2,1)S(1)}, f32[512,1024]{1,0:T(8,128)S(1)}, f32[512,1024]{1,0:T(8,128)S(1)}, f32[384,1024]{1,0:T(8,128)S(1)}, bf16...) custom-call(s32[1,384]{1,0:T(1,128)} %bitcast.12, s32[1,128]{1,0:T(1,128)} %bitcast.13, ...), custom_call_target="tpu_custom_call" | custom-call | flops 20000000000 | bytes 30000000 | tf_op jit(solution)/shard_map/adapter_step/pallas_call | solution.py:474
  81.0 2.6 %hand_over.1 = (bf16[384,1024]{1,0:T(8,128)(2,1)}, bf16[48,8192]{1,0:T(8,128)(2,1)}, f32[512,1024]{1,0:T(8,128)}, f32[512,1024]{1,0:T(8,128)}) custom-call(bf16[48,8192]{1,0:T(8,128)(2,1)S(1)} %get-tuple-element.14.ig, f32[512,1024]{1,0:T(8,128)S(1)} %get-tuple-element.15.da, f32[512,1024]{1,0:T(8,128)S(1)} %get-tuple-element.16.db, ...), custom_call_target="tpu_custom_call" | custom-call | tf_op jit(solution)/shard_map/hand_over/pallas_call | solution.py:528

commit v5 on v4

--- a/solution.py
+++ b/solution.py
@@ -50,12 +50,17 @@
         )
 
     def exchange(send, recv, ss, rs):
+        def at(k):
+            dx, dy = OFFSETS[k]
+            ex, ey = (4 - dx) % 4, (4 - dy) % 4
+            return (x + dx + (ex - dx) * c) % 4 * 4 + (y + dy + (ey - dy) * c) % 4
+
         return [
             remote(
-                send.at[dp_at(k), pl.ds(16 * r, 16)], recv.at[s, pl.ds(16 * r, 16)], ss, rs,
-                {"dp": dp_at(k), "mp": m},
+                send.at[at(k), :, pl.ds(256 * r, 256)], recv.at[s, :, pl.ds(256 * r, 256)], ss, rs,
+                {"dp": at(k), "mp": m},
             )
-            for r in range(3)
+            for r in range(4)
             for k in range(15)
         ]
 
@@ -99,8 +104,6 @@
         capacity = slots // 128
         dest = storage * capacity + jnp.sum(before * hit, axis=1, keepdims=True)
         dest_row = jnp.sum(jnp.where(rr == cc, dest, 0.0), axis=0, keepdims=True)
-        wide = lax.broadcasted_iota(i32, (tok_rows, slots), 1).astype(f32)
-        pt[...] = (wide == dest).astype(f32).astype(bf16)
         tall = lax.broadcasted_iota(i32, (slots, tok_rows), 0).astype(f32)
         pm[...] = (tall == dest_row).astype(f32).astype(bf16)
 
@@ -139,6 +142,8 @@
         copy.start()
     with jax.named_scope("place_tok"):
         place(xall.at[m], sendx)
+        wide = lax.broadcasted_iota(i32, (tok_rows, slots), 1).astype(f32)
+        pt[...] = (wide == dest).astype(f32).astype(bf16)
         recvx[s] = sendx[s]
 
     def pair(j):

time: 83.7 us -> 83.6 us (level)
  no operation moved by 1% of the time
where the time goes in v5:
time: 83.6 us; the launch traced here: 83.5 us
  Pallas kernels  82.8 us (99%)
    pallas_call x1, Pallas kernels, local(): pl.pallas_call(kernel, out_shape=(pltpu.VMEM((own, 8 * cols), bf16), pltp...  80.2 us
    pallas_call x1, Pallas kernels, local(): pl.pallas_call(hand_over, out_shape=(jax.ShapeDtypeStruct(tokens.shape, b...  2.59 us

profile of v5, /device:TPU:1, one launch (start us, length us, event | category | flops | bytes accessed | tf_op | source)
XLA Modules:
  0.0 83.5 jit_solution(8973668146706787340)
XLA Ops:
  0.6 80.2 %adapter_step.1 = (bf16[48,8192]{1,0:T(8,128)(2,1)S(1)}, f32[512,1024]{1,0:T(8,128)S(1)}, f32[512,1024]{1,0:T(8,128)S(1)}, f32[384,1024]{1,0:T(8,128)S(1)}, bf16...) custom-call(s32[1,384]{1,0:T(1,128)} %bitcast.12, s32[1,128]{1,0:T(1,128)} %bitcast.13, ...), custom_call_target="tpu_custom_call" | custom-call | flops 20000000000 | bytes 30000000 | tf_op jit(solution)/shard_map/adapter_step/pallas_call | solution.py:479
  80.9 2.6 %hand_over.1 = (bf16[384,1024]{1,0:T(8,128)(2,1)}, bf16[48,8192]{1,0:T(8,128)(2,1)}, f32[512,1024]{1,0:T(8,128)}, f32[512,1024]{1,0:T(8,128)}) custom-call(bf16[48,8192]{1,0:T(8,128)(2,1)S(1)} %get-tuple-element.14.ig, f32[512,1024]{1,0:T(8,128)S(1)} %get-tuple-element.15.da, f32[512,1024]{1,0:T(8,128)S(1)} %get-tuple-element.16.db, ...), custom_call_target="tpu_custom_call" | custom-call | tf_op jit(solution)/shard_map/hand_over/pallas_call | solution.py:533
